TPU v7x, 32 devices: a whole 2x2x4 slice. The times are simulated.
32 devices in a mesh: box: 8 (over z, core), samp: 4 (over y, x).
Axes of the slice: x: 2, y: 2, z: 4, core: 2. Of those that a mesh axis runs over, the one named last changes fastest.
Arguments:
- radiation: float32 [2, 256, 88, 168], P(None, 'box', 'samp'), may hold values from -6 to 6
- theta_mid: float32 [160, 88], replicated, may hold values from -0.625 to 0.625
- phi_mid: float32 [312, 168], replicated, may hold values from -0.5 to 0.5
- theta_top: float32 [296, 160], replicated, may hold values from -0.5 to 0.5
- phi_top: float32 [584, 312], replicated, may hold values from -0.3125 to 0.3125
- shift_mid: float32 [8, 160, 312], replicated, may hold values from -3.140625 to 3.140625
- shift_top: float32 [8, 296, 584], replicated, may hold values from -3.140625 to 3.140625
- octant_low: int32 [256], P('box'), may hold values from 0 to 7
- octant_mid: int32 [64], P('box'), may hold values from 0 to 7
- parent_low: int32 [256], P('box'), may hold values from 0 to 63, as said below
- parent_mid: int32 [64], P('box'), may hold values from 0 to 15, as said below
- trans_low: float32 [2, 16, 88, 168], P(None, None, 'samp'), may hold values from -4 to 4
- trans_mid: float32 [2, 16, 160, 312], P(None, None, 'samp'), may hold values from -4 to 4
- trans_top: float32 [2, 16, 296, 584], P(None, None, 'samp'), may hold values from -4 to 4
- far_low: int32 [256, 16], P('box'), may hold values from 0 to 255, as said below
- far_mid: int32 [64, 16], P('box'), may hold values from 0 to 63, as said below
- far_top: int32 [16, 16], P('box'), may hold values from 0 to 15, as said below
- offset_low: int32 [256, 16], P('box'), may hold values from 0 to 15
- offset_mid: int32 [64, 16], P('box'), may hold values from 0 to 15
- offset_top: int32 [16, 16], P('box'), may hold values from 0 to 15
Outputs:
- incoming: float32 [2, 256, 88, 168], P(None, 'box', 'samp')
Inputs may be any that keep to these rules, and one draw needn't show every extreme that they name: `parent_low`: each middle box has exactly 4 children; the children of the middle boxes 8 * j to 8 * j + 7 are the finest boxes 32 * j to 32 * j + 31. `parent_mid`: each top box has exactly 4 children; the children of the top boxes 2 * j to 2 * j + 1 are the middle boxes 8 * j to 8 * j + 7. `far_low`: A finest box in the run 32 * j to 32 * j + 31 names only boxes of the runs j - 1, j and j + 1 (those that exist); every box whose run has a lower neighbour run names a box of it, and likewise for a higher one. `far_mid`: A middle box in the run 8 * j to 8 * j + 7 names only boxes of the runs j - 1, j and j + 1 (those that exist); every box whose run has a lower neighbour run names a box of it, and likewise for a higher one. `far_top`: A top box in the run 2 * j to 2 * j + 1 names only boxes of the runs j - 1, j and j + 1 (those that exist); every box whose run has a lower neighbour run names a box of it, and likewise for a higher one.
All inputs are finite; a program needn't handle non-finite values.
Results may differ from a plain program's by a relative error of at most 0.000071.
Values sent between devices are 32-bit elements; how exact they have to be, the bound alone decides.
A program may use at most 192 MiB of HBM per device.

v0:
```python
import jax
import jax.numpy as jnp
from jax import lax
from jax.sharding import PartitionSpec as P

highest = lax.Precision.HIGHEST


def extended(block, sides, width):
    for axis, dim in sides:
        count = lax.axis_size(axis)
        forward = [(i, i + 1) for i in range(count - 1)]
        backward = [(target, source) for source, target in forward]
        low = lax.ppermute(
            lax.slice_in_dim(block, block.shape[dim] - width, None, axis=dim), axis, forward
        )
        high = lax.ppermute(lax.slice_in_dim(block, 0, width, axis=dim), axis, backward)
        block = jnp.concatenate([low, block, high], axis=dim)
    return block


def rotate(real_part, imag_part, cosines, sines):
    return (real_part * cosines - imag_part * sines, real_part * sines + imag_part * cosines)


def shift_pattern(patterns, angle_rows, octant, factor):
    cosines = jnp.take(jnp.cos(angle_rows), octant, axis=0)
    sines = factor * jnp.take(jnp.sin(angle_rows), octant, axis=0)
    real_part, imag_part = rotate(patterns[0], patterns[1], cosines, sines)
    return jnp.stack([real_part, imag_part])


def parent_table(parent, parents_here):
    within = parent - lax.axis_index("box") * parents_here
    return (within[:, None] == jnp.arange(parents_here, dtype=jnp.int32)[None, :]).astype(
        jnp.float32
    )


def aggregate(height, patterns, theta_w, phi_w, angles, octant, parent, parents_here):
    interp = jnp.einsum("rbtp,qp->rbtq", patterns, phi_w, precision=highest)
    rows_parent = theta_w.shape[0] // lax.axis_size("samp")
    sample_idx = lax.axis_index("samp")
    theta_own = lax.dynamic_slice_in_dim(theta_w, sample_idx * rows_parent, rows_parent, 0)

    def add_rows(running, portion, anchor):
        return jnp.einsum("st,rbtq->rbsq", theta_own, portion, precision=highest)

    initial = jnp.zeros((2, patterns.shape[1], rows_parent, phi_w.shape[0]), jnp.float32)
    if height == 1:
        mixed = add_rows(initial, lax.all_gather(interp, "samp", axis=2, tiled=True), jnp.int32(0))
    else:
        mixed = add_rows(initial, lax.all_gather(interp, "samp", axis=2, tiled=True), jnp.int32(0))
    angle_rows = lax.dynamic_slice_in_dim(angles, sample_idx * rows_parent, rows_parent, 1)
    shifted = shift_pattern(mixed, angle_rows, octant, 1.0)
    return jnp.einsum(
        "cp,rcsq->rpsq", parent_table(parent, parents_here), shifted, precision=highest
    )


def disaggregate(height, patterns, theta_w, phi_w, angles, octant, parent):
    rows_child = theta_w.shape[1] // lax.axis_size("samp")
    sample_idx = lax.axis_index("samp")
    parent_hot = parent_table(parent, patterns.shape[1])
    theta_cols = lax.dynamic_slice_in_dim(theta_w, sample_idx * rows_child, rows_child, 1)

    def add_rows(running, portion, anchor):
        spread = jnp.einsum("cp,rpsq->rcsq", parent_hot, portion, precision=highest)
        shifted = shift_pattern(spread, angles, octant, -1.0)
        return jnp.einsum("st,rcsq->rctq", theta_cols, shifted, precision=highest)

    initial = jnp.zeros((2, parent.shape[0], rows_child, patterns.shape[3]), jnp.float32)
    if height == 1:
        mixed = add_rows(
            initial, lax.all_gather(patterns, "samp", axis=2, tiled=True), jnp.int32(0)
        )
    else:
        mixed = add_rows(
            initial, lax.all_gather(patterns, "samp", axis=2, tiled=True), jnp.int32(0)
        )
    return jnp.einsum("rctq,qp->rctp", mixed, phi_w, precision=highest)


def near_runs(section, patterns):
    width = patterns.shape[1]
    if section == 0:
        return extended(patterns, (("box", 1),), width)
    if section == 1:
        return extended(patterns, (("box", 1),), width)
    return extended(patterns, (("box", 1),), width)


def translate_local(padded, table, local_ids, offsets, shape):

    def advance(running, columns):
        id_col, off_col = columns
        sources = jnp.take(padded, id_col, axis=1)
        coeffs = jnp.take(table, off_col, axis=1)
        real_part, imag_part = rotate(sources[0], sources[1], coeffs[0], coeffs[1])
        return (running + jnp.stack([real_part, imag_part]), None)

    initial = jnp.zeros(shape, jnp.float32)
    result, _ = lax.scan(advance, initial, (local_ids.T, offsets.T))
    return result


def body(
    radiation,
    theta_mid,
    phi_mid,
    theta_top,
    phi_top,
    shift_mid,
    shift_top,
    octant_low,
    octant_mid,
    parent_low,
    parent_mid,
    trans_low,
    trans_mid,
    trans_top,
    far_low,
    far_mid,
    far_top,
    offset_low,
    offset_mid,
    offset_top,
):
    boxes_low = radiation.shape[1]
    middle = aggregate(
        1, radiation, theta_mid, phi_mid, shift_mid, octant_low, parent_low, boxes_low // 4
    )
    summit = aggregate(
        2, middle, theta_top, phi_top, shift_top, octant_mid, parent_mid, boxes_low // 16
    )
    far_lists = (far_low, far_mid, far_top)
    offset_lists = (offset_low, offset_mid, offset_top)
    tables = (trans_low, trans_mid, trans_top)
    locals_here = (radiation, middle, summit)
    results = []
    for section in range(3):
        here = locals_here[section]
        padded = near_runs(section, here)
        first_box = (lax.axis_index("box") - 1) * here.shape[1]
        local_ids = far_lists[section] - first_box
        results.append(
            translate_local(padded, tables[section], local_ids, offset_lists[section], here.shape)
        )
    in_low, in_mid, in_top = (results[0], results[1], results[2])
    in_mid = in_mid + disaggregate(2, in_top, theta_top, phi_top, shift_top, octant_mid, parent_mid)
    return in_low + disaggregate(1, in_mid, theta_mid, phi_mid, shift_mid, octant_low, parent_low)


def solution(mesh):
    in_specs = (
        P(None, "box", "samp", None),
        P(),
        P(),
        P(),
        P(),
        P(),
        P(),
        P("box"),
        P("box"),
        P("box"),
        P("box"),
        P(None, None, "samp", None),
        P(None, None, "samp", None),
        P(None, None, "samp", None),
        P("box", None),
        P("box", None),
        P("box", None),
        P("box", None),
        P("box", None),
        P("box", None),
    )
    out_specs = P(None, "box", "samp", None)
    return jax.shard_map(body, mesh=mesh, in_specs=in_specs, out_specs=out_specs, check_vma=False)
```

profile of v0, /device:TPU:8, one launch (start us, length us, event | category | flops | bytes accessed | tf_op | source)
XLA Modules:
  0.0 970.3 jit_solution(5403001865971188087)
XLA Ops:
  6.5 5.2 fusion.29
  19.0 83.9 %all-gather.5.cloned.1.call-done = f32[2,32,88,312]{3,1,0,2:T(8,128)} async-done(((f32[2,32,22,312]{3,1,0,2:T(8,128)}), f32[2,32,88,312]{3,1,0,2:T(8,128)}) %all-gather.5.cloned.1.call-update) | async-done | bytes 7028752 | tf_op jit(solution)/shard_map/all_gather | solution.py:51
  102.9 13.9 %fusion.21 = f32[2,32,40,312]{3,2,1,0:T(8,128)S(1)} fusion(f32[2,32,88,312]{3,1,0,2:T(8,128)} %all-gather.5.cloned.1.call-done, f32[160,88]{1,0:T(8,128)} %param.35, s32[]{:T(128)S(6)} %select_n.153), kind=kOutput, calls=%fused_computation.101 | convolution fusion | flops 843448320 | bytes 11866116 | tf_op jit(solution)/shard_map/st,rbtq->rbsq/dot_general | solution.py:47
  120.4 4.2 fusion.40
  132.5 8.7 dynamic-slice_cosine_fusion
  146.5 9.9 %copy.107 = f32[2,16,74,584]{3,0,2,1:T(2,128)} copy(f32[2,16,74,584]{3,1,2,0:T(8,128)} %param.47) | data formatting | bytes 11063296
  156.5 23.3 %fusion.71 = (f32[8,296,584]{2,1,0:T(8,128)}, f32[8,296,584]{2,1,0:T(8,128)}) fusion(f32[8,296,584]{2,1,0:T(8,128)} %param.40), kind=kLoop, calls=%fused_computation.162 | loop fusion | bytes 16594944 | tf_op jit(solution)/shard_map/sin | solution.py:28
  179.8 6.3 gather_fusion.10
  186.1 6.2 gather_fusion.11
  192.4 10.7 %fusion.72 = (f32[8,160,312]{2,1,0:T(8,128)S(1)}, f32[8,160,312]{2,1,0:T(8,128)}) fusion(f32[8,160,312]{2,1,0:T(8,128)} %param.39), kind=kLoop, calls=%fused_computation.163 | loop fusion | bytes 4792320 | tf_op jit(solution)/shard_map/sin | solution.py:28
  203.2 5.7 gather_fusion.12
  220.5 6.3 convolution_bitcast_fusion.2
  235.6 5.9 pad_maximum_fusion.2
  248.9 191.7 %while.35 = (s32[]{:T(128)}, f32[2,2,74,584]{3,0,2,1:T(2,128)}, s32[16,2]{1,0:T(8,128)S(1)}, f32[2,6,74,584]{3,0,2,1:T(2,128)}, s32[16,2]{1,0:T(8,128)S(1)}, /*i...) while((s32[]{:T(128)}, f32[2,2,74,584]{3,0,2,1:T(2,128)}, s32[16,2]{1,0:T(8,128)S(1)}, ...), condition=%wide.region_5.8_spmd.clone, body=%wide.region_4.7_spmd.clone.sunk | while | flops 1384999 | bytes 9688767 | solution.py:103
  259.9 4.2 gather_fusion.4
  271.9 4.2 gather_fusion.4
  296.0 4.2 gather_fusion.4
  308.1 4.2 gather_fusion.4
  320.2 4.2 gather_fusion.4
  356.3 4.2 gather_fusion.4
  368.4 4.2 gather_fusion.4
  380.4 4.2 gather_fusion.4
  416.6 4.2 gather_fusion.4
  443.2 118.3 %while.34 = (s32[]{:T(128)}, f32[2,8,40,312]{3,2,0,1:T(8,128)}, s32[16,8]{1,0:T(8,128)S(1)}, f32[2,24,40,312]{3,2,1,0:T(8,128)}, s32[16,8]{1,0:T(8,128)S(1)}, /*...) while((s32[]{:T(128)}, f32[2,8,40,312]{3,2,0,1:T(8,128)}, s32[16,8]{1,0:T(8,128)S(1)}, ...), condition=%wide.region_3.5_spmd.clone, body=%wide.region_2.4_spmd.clone.sunk | while | flops 1599635 | bytes 11190727 | solution.py:103
  561.5 8.6 convolution_bitcast_fusion.1
  570.1 19.3 %subtract_bitcast_fusion.1 = (f32[1,8,296,584]{3,1,2,0:T(8,128)}, f32[1,8,296,584]{3,1,2,0:T(8,128)}) fusion(f32[2,8,296,584]{3,1,2,0:T(8,128)S(1)} %convolution_bitcast_fusion.1, f32[8,296,584]{2,1,0:T(8,128)} %gather_fusion.10, f32[8,296,584]{2,1,0:T(8,128)} %gather_fusion.11, pred[8]{0:T(512)(128)(4,1)S(1)} %compare_and_fusion.6), kind=kLoop, calls=%fused_computation.87 | loop fusion | flops 12446208 | bytes 33189896 | tf_op jit(solution)/shard_map/stack | solution.py:30
  589.4 9.6 pad_maximum_fusion.1
  599.0 14.0 %fusion.8 = f32[2,8,584,40]{2,3,1,0:T(8,128)S(1)} fusion(f32[2,8,296,584]{3,1,2,0:T(8,128)} %pad_maximum_fusion.1, f32[296,160]{0,1:T(8,128)} %param.37, s32[]{:T(128)S(6)} %select_n.153), kind=kOutput, calls=%fused_computation.69 | convolution fusion | flops 1327595520 | bytes 13680644 | tf_op jit(solution)/shard_map/st,rcsq->rctq/dot_general | solution.py:70
  617.0 275.0 %while.33 = (s32[]{:T(128)}, f32[2,32,22,168]{3,0,2,1:T(2,128)}, s32[16,32]{1,0:T(8,128)S(1)}, f32[2,96,22,168]{3,0,2,1:T(2,128)}, s32[16,32]{1,0:T(8,128)}, /*i...) while((s32[]{:T(128)}, f32[2,32,22,168]{3,0,2,1:T(2,128)}, s32[16,32]{1,0:T(8,128)S(1)}, ...), condition=%wide.region_1.2_spmd.clone, body=%wide.region_0.1_spmd.clone.sunk | while | flops 1894979 | bytes 17040900 | solution.py:103
  622.8 4.7 gather_fusion.1
  639.1 4.3 gather_fusion.1
  646.7 4.3 maximum_add_fusion.6
  656.3 4.3 gather_fusion.1
  663.9 4.3 maximum_add_fusion.6
  673.5 4.3 gather_fusion.1
  681.1 4.3 maximum_add_fusion.6
  690.8 4.3 gather_fusion.1
  698.3 4.3 maximum_add_fusion.6
  708.0 4.3 gather_fusion.1
  715.6 4.3 maximum_add_fusion.6
  725.2 4.3 gather_fusion.1
  732.8 4.3 maximum_add_fusion.6
  742.4 4.3 gather_fusion.1
  750.0 4.3 maximum_add_fusion.6
  759.7 4.3 gather_fusion.1
  767.2 4.3 maximum_add_fusion.6
  776.9 4.3 gather_fusion.1
  784.5 4.3 maximum_add_fusion.6
  794.1 4.3 gather_fusion.1
  801.7 4.3 maximum_add_fusion.6
  811.3 4.3 gather_fusion.1
  818.9 4.3 maximum_add_fusion.6
  828.5 4.3 gather_fusion.1
  836.1 4.3 maximum_add_fusion.6
  845.8 4.3 gather_fusion.1
  853.4 4.3 maximum_add_fusion.6
  863.0 4.3 gather_fusion.1
  870.6 4.3 maximum_add_fusion.6
  880.2 4.3 gather_fusion.1
  887.8 4.3 maximum_add_fusion.6
  892.1 12.4 %convolution_bitcast_fusion = f32[2,32,160,312]{3,1,2,0:T(8,128)} fusion(f32[2,8,160,312]{3,2,1,0:T(8,128)} %all-gather.11.cloned.1.call-done, s32[32]{0:T(128)S(1)} %broadcast_subtract_fusion.1), kind=kOutput, calls=%fused_computation.80 | convolution fusion | flops 306708736 | bytes 15974528 | tf_op jit(solution)/shard_map/cp,rpsq->rcsq/dot_general | solution.py:68
  904.5 21.3 %subtract_bitcast_fusion = (f32[1,32,160,312]{3,1,2,0:T(8,128)}, f32[1,32,160,312]{3,1,2,0:T(8,128)}) fusion(f32[2,32,160,312]{3,1,2,0:T(8,128)} %convolution_bitcast_fusion, f32[32,160,312]{2,1,0:T(8,128)} %gather_fusion.12, f32[32,160,312]{2,1,0:T(8,128)} %gather_fusion.13, pred[32]{0:T(512)(128)(4,1)S(1)} %copy-done.17), kind=kLoop, calls=%fused_computation.79 | loop fusion | flops 14376960 | bytes 38338592 | tf_op jit(solution)/shard_map/stack | solution.py:30
  925.7 12.7 %pad_maximum_fusion = f32[2,32,160,312]{3,1,2,0:T(8,128)} fusion(f32[1,32,160,312]{3,1,2,0:T(8,128)} %get-tuple-element.292, f32[1,32,160,312]{3,1,2,0:T(8,128)} %get-tuple-element.291), kind=kLoop, calls=%fused_computation.65 | loop fusion | flops 3194880 | bytes 25559040 | tf_op jit(solution)/shard_map/stack | solution.py:30
  938.4 21.5 %fusion.24 = f32[2,32,22,312]{3,2,1,0:T(8,128)S(1)} fusion(f32[2,32,160,312]{3,1,2,0:T(8,128)} %pad_maximum_fusion, f32[160,88]{1,0:T(8,128)S(1)} %copy-done.12, s32[]{:T(128)S(6)} %select_n.155), kind=kOutput, calls=%fused_computation.107 | convolution fusion | flops 843448320 | bytes 14593028 | tf_op jit(solution)/shard_map/st,rcsq->rctq/dot_general | solution.py:70
  (580 shorter events, 472.0 us)
Async XLA Ops:
  6.5 113.9 %copy-start = (f32[584,312]{0,1:T(8,128)S(1)}, f32[584,312]{0,1:T(8,128)}, u32[]{:S(2)}) copy-start(f32[584,312]{0,1:T(8,128)} %param.38) | copy-start | bytes 2186500
  6.5 5.3 copy-start.20
  6.5 96.4 %all-gather.5.cloned.1.call-start = ((), (), s32[]{:S(2)}) async-start(), calls=%async_computation | async-start | bytes 10813440 | tf_op jit(solution)/shard_map/all_gather | solution.py:51
  11.8 208.7 %all-gather.7.cloned.1.call-start = ((), (), s32[]{:S(2)}) async-start(), calls=%async_computation.1 | async-start | bytes 8192000 | tf_op jit(solution)/shard_map/all_gather | solution.py:53
  14.9 4.0 copy-start.21
  19.0 97.8 %copy-start.16 = (pred[32]{0:T(512)(128)(4,1)}, pred[32]{0:T(512)(128)(4,1)S(1)}, u32[]{:S(2)}) copy-start(pred[32]{0:T(512)(128)(4,1)S(1)} %compare_and_fusion.7) | copy-start | bytes 100
  19.0 97.8 %copy-start.6 = (f32[32,40,312]{2,1,0:T(8,128)S(1)}, f32[32,40,312]{2,1,0:T(8,128)}, u32[]{:S(2)}) copy-start(f32[32,40,312]{2,1,0:T(8,128)} %gather_fusion.6) | copy-start | bytes 4792324
  102.9 13.9 %copy-start.7 = (f32[32,40,312]{2,1,0:T(8,128)S(1)}, f32[32,40,312]{2,1,0:T(8,128)}, u32[]{:S(2)}) copy-start(f32[32,40,312]{2,1,0:T(8,128)} %gather_fusion.7) | copy-start | bytes 4792324
  119.4 1.0 copy-start.4
  120.4 4.3 copy-start.10
  124.6 7.9 copy-start.22
  124.6 436.9 %all-gather.9.cloned.1.call-start = ((), (), s32[]{:S(2)}) async-start(), calls=%async_computation.2 | async-start | bytes 3788800 | tf_op jit(solution)/shard_map/all_gather | solution.py:79
  126.9 105.0 %collective-permute-start = (f32[2,32,22,168]{3,0,2,1:T(2,128)}, f32[2,32,22,168]{3,0,2,1:T(2,128)}, u32[]{:S(2)}, u32[]{:S(2)}) collective-permute-start(f32[2,32,22,168]{3,0,2,1:T(2,128)} %copy.90), channel_id=1, source_target_pairs={{0,4},{4,8},{8,12},{12,16},{16,20},{20,24},{24,28},{1,5},{5,9},{9,... | collective-permute-start | bytes 2838536 | tf_op jit(solution)/shard_map/ppermute | solution.py:14
  128.8 106.7 %collective-permute-start.1 = (f32[2,32,22,168]{3,0,2,1:T(2,128)}, f32[2,32,22,168]{3,0,2,1:T(2,128)}, u32[]{:S(2)}, u32[]{:S(2)}) collective-permute-start(f32[2,32,22,168]{3,0,2,1:T(2,128)} %copy.90), channel_id=1, source_target_pairs={{4,0},{8,4},{12,8},{16,12},{20,16},{24,20},{28,24},{5,1},{9,5},{13... | collective-permute-start | bytes 2838536 | tf_op jit(solution)/shard_map/ppermute | solution.py:17
  141.3 5.1 copy-start.19
  146.5 9.9 %copy-start.18 = (s32[2,16]{1,0:T(2,128)S(1)}, s32[2,16]{1,0:T(2,128)}, u32[]{:S(2)}) copy-start(s32[2,16]{1,0:T(2,128)} %param.53) | copy-start | bytes 388
  186.1 6.2 copy-start.15
  186.1 6.3 copy-start.14
  208.9 5.8 copy-start.23
  208.9 5.8 copy-start.13
  214.7 12.1 %copy-start.8 = (f32[8,74,584]{2,1,0:T(8,128)S(1)}, f32[8,74,584]{2,1,0:T(8,128)}, u32[]{:S(2)}) copy-start(f32[8,74,584]{2,1,0:T(8,128)} %gather_fusion.8) | copy-start | bytes 4148740
  214.7 26.7 %collective-permute-start.2 = (f32[2,8,40,312]{3,1,2,0:T(8,128)}, f32[2,8,40,312]{3,1,2,0:T(8,128)}, u32[]{:S(2)}, u32[]{:S(2)}) collective-permute-start(f32[2,8,40,312]{3,1,2,0:T(8,128)} %copy-done.4), channel_id=1, source_target_pairs={{0,4},{4,8},{8,12},{12,16},{16,20},{20,24},{24,28},{1,5},{5,9},{9,... | collective-permute-start | bytes 2396168 | tf_op jit(solution)/shard_map/ppermute | solution.py:14
  216.8 24.7 %collective-permute-start.3 = (f32[2,8,40,312]{3,1,2,0:T(8,128)}, f32[2,8,40,312]{3,1,2,0:T(8,128)}, u32[]{:S(2)}, u32[]{:S(2)}) collective-permute-start(f32[2,8,40,312]{3,1,2,0:T(8,128)} %copy-done.4), channel_id=1, source_target_pairs={{4,0},{8,4},{12,8},{16,12},{20,16},{24,20},{28,24},{5,1},{9,5},{13... | collective-permute-start | bytes 2396168 | tf_op jit(solution)/shard_map/ppermute | solution.py:17
  220.5 6.3 copy-start.9
  229.8 11.7 %copy-start.5 = (f32[2,8,40,312]{3,1,2,0:T(8,128)S(1)}, f32[2,8,40,312]{3,1,2,0:T(8,128)}, u32[]{:S(2)}) copy-start(f32[2,8,40,312]{3,1,2,0:T(8,128)} %copy-done.4) | copy-start | bytes 2396164
  229.8 15.6 %collective-permute-start.4 = (f32[2,2,74,584]{3,1,2,0:T(2,128)S(1)}, f32[2,2,74,584]{3,1,2,0:T(2,128)S(1)}, u32[]{:S(2)}, u32[]{:S(2)}) collective-permute-start(f32[2,2,74,584]{3,1,2,0:T(2,128)S(1)} %fusion.37), channel_id=1, source_target_pairs={{0,4},{4,8},{8,12},{12,16},{16,20},{20,24},{24,28},{1,5},{5,9},{9,... | collective-permute-start | bytes 2074376 | tf_op jit(solution)/shard_map/ppermute | solution.py:14
  231.9 13.5 %collective-permute-start.5 = (f32[2,2,74,584]{3,1,2,0:T(2,128)S(1)}, f32[2,2,74,584]{3,1,2,0:T(2,128)S(1)}, u32[]{:S(2)}, u32[]{:S(2)}) collective-permute-start(f32[2,2,74,584]{3,1,2,0:T(2,128)S(1)} %fusion.37), channel_id=1, source_target_pairs={{4,0},{8,4},{12,8},{16,12},{20,16},{24,20},{28,24},{5,1},{9,5},{13... | collective-permute-start | bytes 2074376 | tf_op jit(solution)/shard_map/ppermute | solution.py:17
  443.1 449.0 %all-gather.11.cloned.1.call-start = ((), (), s32[]{:S(2)}) async-start(), calls=%async_computation.3 | async-start | bytes 4915200 | tf_op jit(solution)/shard_map/all_gather | solution.py:75
  599.0 14.0 %copy-start.3 = (f32[2,8,40,312]{3,2,0,1:T(8,128)S(1)}, f32[2,8,40,312]{3,2,0,1:T(8,128)}, u32[]{:S(2)}) copy-start(f32[2,8,40,312]{3,2,0,1:T(8,128)} %get-tuple-element.106) | copy-start | bytes 2396164
  627.6 1.4 copy-start.1
  643.4 1.4 copy-start.1
  660.6 1.4 copy-start.1
  677.9 1.4 copy-start.1
  695.1 1.4 copy-start.1
  712.3 1.4 copy-start.1
  729.5 1.4 copy-start.1
  746.8 1.4 copy-start.1
  764.0 1.4 copy-start.1
  781.2 1.4 copy-start.1
  798.4 1.4 copy-start.1
  815.6 1.4 copy-start.1
  832.9 1.4 copy-start.1
  850.1 1.4 copy-start.1
  867.3 1.4 copy-start.1
  884.5 1.4 copy-start.1
  892.1 12.4 %copy-start.17 = (pred[32]{0:T(512)(128)(4,1)S(1)}, pred[32]{0:T(512)(128)(4,1)}, u32[]{:S(2)}) copy-start(pred[32]{0:T(512)(128)(4,1)} %copy-done.16) | copy-start | bytes 100
  925.7 12.7 %copy-start.12 = (f32[160,88]{1,0:T(8,128)S(1)}, f32[160,88]{1,0:T(8,128)}, u32[]{:S(2)}) copy-start(f32[160,88]{1,0:T(8,128)} %param.35) | copy-start | bytes 168964
  938.4 21.6 %copy-start.2 = (f32[2,32,22,168]{3,0,2,1:T(2,128)S(1)}, f32[2,32,22,168]{3,0,2,1:T(2,128)}, u32[]{:S(2)}) copy-start(f32[2,32,22,168]{3,0,2,1:T(2,128)} %get-tuple-element.105) | copy-start | bytes 2838532
  938.4 21.6 %copy-start.11 = (f32[312,168]{0,1:T(8,128)S(1)}, f32[312,168]{0,1:T(8,128)}, u32[]{:S(2)}) copy-start(f32[312,168]{0,1:T(8,128)} %param.36) | copy-start | bytes 628996
Sparse Core Ops, SparseCore 0:
  11.9 90.9 all-gather.4
  124.8 72.3 all-gather.6
  443.2 43.0 all-gather.8
  617.2 50.5 all-gather.10
where the time goes:
time: 986 us; the launch traced here: 970 us
  local copies, waits for them, and re-layouts  402 us (41%)
  other arithmetic  352 us (36%)
  matrix products  97.6 us (10%)
  waiting for transfers between devices  84 us (9%)
  starting transfers between devices  17.1 us (2%)
  between operations  13.8 us (1%)
    gather x48, local copies, waits for them, and re-layouts, advance(): sources = jnp.take(padded, id_col, axis=1)  158 us
    add x48, other arithmetic, advance(): return (running + jnp.stack([real_part, imag_part]), None)  149 us
    gather x48, local copies, waits for them, and re-layouts, advance(): coeffs = jnp.take(table, off_col, axis=1)  135 us
    all_gather x2, waiting for transfers between devices, aggregate(): lax.all_gather(interp, 'samp', axis=2, tiled=True)  83.9 us
    another operation x8, other arithmetic, shift_pattern(): return jnp.stack([real_part, imag_part])  64.5 us
    sub x48, other arithmetic, rotate(): real_part * cosines - imag_part * sines  47.5 us
    select_n x48, other arithmetic, advance(): coeffs = jnp.take(table, off_col, axis=1)  37.8 us
    dot_general x2, matrix products, add_rows(): return jnp.einsum('st,rcsq->rctq', theta_cols, shifted, precision=highest)  35.5 us
  transfers between devices with their start and end apart: 10, of which 1 were waited for; matrix products, arithmetic and copies ran while one was open for 51% of the time, Pallas kernels for 0%

commit v1 on v0

v1 whole, which is shorter than its diff:
```python
import functools

import jax
import jax.numpy as jnp
from jax import lax
from jax.experimental import pallas as pl
from jax.experimental.pallas import tpu as pltpu
from jax.sharding import PartitionSpec as P

VMEM_LIMIT = 48 * 1024 * 1024
VMEM = pltpu.VMEM
SMEM = pltpu.SMEM


def sincos(angle):
    half = 0.5 * angle
    z = half * half
    s = jnp.float32(1.0 / 6227020800.0)
    for c in (-1.0 / 39916800.0, 1.0 / 362880.0, -1.0 / 5040.0, 1.0 / 120.0, -1.0 / 6.0, 1.0):
        s = s * z + c
    s = s * half
    k = jnp.float32(1.0 / 479001600.0)
    for c in (-1.0 / 3628800.0, 1.0 / 40320.0, -1.0 / 720.0, 1.0 / 24.0, -0.5, 1.0):
        k = k * z + c
    return 2.0 * s * k, 1.0 - 2.0 * s * s


def split(x):
    high = x.astype(jnp.bfloat16)
    return high, (x - high.astype(jnp.float32)).astype(jnp.bfloat16)


def dot3(a, b):
    (ah, al), (bh, bl) = split(a), split(b)
    dot = functools.partial(jnp.dot, preferred_element_type=jnp.float32)
    return dot(ah, bl) + dot(al, bh) + dot(ah, bh)


def up_kernel(n, kids, oct_ref, x_ref, q_ref, rt_ref, shift_ref, out_ref, x_all, mixed):
    i = pl.program_id(0)
    rows = x_ref.shape[3]
    theta = n * rows
    rows_out = out_ref.shape[3]
    for r in range(2):
        for k in range(n):
            x_all[r * theta + k * rows:r * theta + (k + 1) * rows, :] = x_ref[k, r, 0]
    interp = dot3(x_all[...], rt_ref[...])
    q = q_ref[...]
    real = dot3(q, interp[:theta])
    imag = dot3(q, interp[theta:])
    sine, cosine = sincos(shift_ref[0])
    turned = (real * cosine - imag * sine, real * sine + imag * cosine)
    child = lax.rem(i, kids)

    @pl.when(child == 0)
    def _():
        for r in range(2):
            mixed[r] = turned[r]

    @pl.when(child > 0)
    def _():
        for r in range(2):
            mixed[r] = mixed[r] + turned[r]

    @pl.when(child == kids - 1)
    def _():
        for r in range(2):
            for k in range(n):
                out_ref[k, r, 0] = mixed[r, k * rows_out:(k + 1) * rows_out, :]


def go_up(x, theta_w, phi_w, angles, octant, parents):
    n, _, boxes, rows, p = x.shape
    s, q = theta_w.shape[0], phi_w.shape[0]
    kids = boxes // parents
    spec = pltpu.PrefetchScalarGridSpec(
        num_scalar_prefetch=1,
        grid=(boxes,),
        in_specs=[
            pl.BlockSpec((n, 2, 1, rows, p), lambda i, o: (0, 0, i, 0, 0)),
            pl.BlockSpec((s, n * rows), lambda i, o: (0, 0)),
            pl.BlockSpec((p, q), lambda i, o: (0, 0)),
            pl.BlockSpec((1, s, q), lambda i, o: (o[i], 0, 0)),
        ],
        out_specs=pl.BlockSpec((n, 2, 1, s // n, q), lambda i, o: (0, 0, i // kids, 0, 0)),
        scratch_shapes=[
            pltpu.VMEM((2 * n * rows, p), jnp.float32),
            pltpu.VMEM((2, s, q), jnp.float32),
        ],
    )
    return pl.pallas_call(
        functools.partial(up_kernel, n, kids),
        grid_spec=spec,
        out_shape=jax.ShapeDtypeStruct((n, 2, parents, s // n, q), jnp.float32),
        compiler_params=pltpu.CompilerParams(vmem_limit_bytes=VMEM_LIMIT),
    )(octant, x, theta_w, phi_w.T, angles)


def down_kernel(n, kids, with_add, oct_ref, g_ref, qt_ref, r_ref, shift_ref, *rest):
    if with_add:
        add_ref, out_ref, held, mixed, final = rest
    else:
        out_ref, held, mixed, final = rest
    i = pl.program_id(0)
    rows = g_ref.shape[3]
    theta = qt_ref.shape[0]
    rows_out = theta // n

    @pl.when(lax.rem(i, kids) == 0)
    def _():
        for r in range(2):
            for k in range(n):
                held[r, k * rows:(k + 1) * rows, :] = g_ref[k, r, 0]

    sine, cosine = sincos(shift_ref[0])
    real, imag = held[0], held[1]
    qt = qt_ref[...]
    mixed[:theta, :] = dot3(qt, real * cosine + imag * sine)
    mixed[theta:, :] = dot3(qt, imag * cosine - real * sine)
    final[...] = dot3(mixed[...], r_ref[...])
    for r in range(2):
        for k in range(n):
            part = final[r * theta + k * rows_out:r * theta + (k + 1) * rows_out, :]
            out_ref[k, r, 0] = part + add_ref[k, r, 0] if with_add else part


def go_down(g, theta_w, phi_w, angles, octant, add):
    n, _, parents, rows, q = g.shape
    boxes = octant.shape[0]
    kids = boxes // parents
    s, t = theta_w.shape
    p = phi_w.shape[1]
    block_out = pl.BlockSpec((n, 2, 1, t // n, p), lambda i, o: (0, 0, i, 0, 0))
    with_add = add is not None
    spec = pltpu.PrefetchScalarGridSpec(
        num_scalar_prefetch=1,
        grid=(boxes,),
        in_specs=[
            pl.BlockSpec((n, 2, 1, rows, q), lambda i, o: (0, 0, i // kids, 0, 0)),
            pl.BlockSpec((t, s), lambda i, o: (0, 0)),
            pl.BlockSpec((q, p), lambda i, o: (0, 0)),
            pl.BlockSpec((1, s, q), lambda i, o: (o[i], 0, 0)),
        ] + ([block_out] if with_add else []),
        out_specs=block_out,
        scratch_shapes=[
            pltpu.VMEM((2, s, q), jnp.float32),
            pltpu.VMEM((2 * t, q), jnp.float32),
            pltpu.VMEM((2 * t, p), jnp.float32),
        ],
    )
    args = (octant, g, theta_w.T, phi_w, angles) + ((add,) if with_add else ())
    return pl.pallas_call(
        functools.partial(down_kernel, n, kids, with_add),
        grid_spec=spec,
        out_shape=jax.ShapeDtypeStruct((n, 2, boxes, t // n, p), jnp.float32),
        compiler_params=pltpu.CompilerParams(vmem_limit_bytes=VMEM_LIMIT),
    )(*args)


def translate_kernel(boxes, group, noff, with_add, chunk, e_ref, o_ref, *rest):
    if with_add:
        a_ref, pat, tab, add_ref, out_ref = rest
    else:
        pat, tab, out_ref = rest
    rows = pat.shape[1]
    far = e_ref.shape[1]

    def step(b, carry):
        place = (b // group) * (2 * group) + lax.rem(b, group)
        for lo in range(0, rows, chunk):
            here = slice(lo, min(lo + chunk, rows))
            if with_add:
                start = a_ref[b]
                real = add_ref[start, here, :]
                imag = add_ref[start + with_add, here, :]
            else:
                real = imag = None
            for f in range(far):
                e, o = e_ref[b, f], o_ref[b, f]
                sr, si = pat[e, here, :], pat[e + boxes, here, :]
                cr, ci = tab[o, here, :], tab[o + noff, here, :]
                dr, di = sr * cr - si * ci, sr * ci + si * cr
                real = dr if real is None else real + dr
                imag = di if imag is None else imag + di
            out_ref[place, here, :] = real
            out_ref[place + group, here, :] = imag
        return carry

    lax.fori_loop(0, boxes, step, 0)


def translate(near, table, far_ids, offsets, group, add=None, add_at=None, add_group=0):
    _, _, boxes, rows, p = near.shape
    noff = table.shape[1]
    chunk = 24 if p <= 256 else 16 if p <= 384 else 8
    first = (lax.axis_index("box") - 1) * boxes
    local = far_ids - first
    entry = (local // boxes) * (2 * boxes) + local % boxes
    args = [entry, offsets]
    specs = [pl.BlockSpec(memory_space=SMEM)] * 2
    if add is not None:
        args.append((add_at // add_group) * (2 * add_group) + add_at % add_group)
        specs.append(pl.BlockSpec(memory_space=SMEM))
    args += [near.reshape(6 * boxes, rows, p), table.reshape(2 * noff, rows, p)]
    specs += [pl.BlockSpec(memory_space=VMEM)] * 2
    if add is not None:
        args.append(add.reshape(-1, rows, p))
        specs.append(pl.BlockSpec(memory_space=VMEM))
    out = pl.pallas_call(
        functools.partial(translate_kernel, boxes, group, noff, add_group, chunk),
        in_specs=specs,
        out_specs=pl.BlockSpec(memory_space=VMEM),
        out_shape=jax.ShapeDtypeStruct((2 * boxes, rows, p), jnp.float32),
        compiler_params=pltpu.CompilerParams(vmem_limit_bytes=VMEM_LIMIT),
    )(*args)
    return out.reshape(boxes // group, 2, group, rows, p)


def exchange_kernel(n, runs, swaps, halos, shares, *refs):
    count = swaps + halos
    xs, ys = refs[:count], refs[count:2 * count]
    send, recv, own, halo_send, halo_recv = refs[2 * count:]
    me = lax.axis_index("samp")
    box = lax.axis_index("box")
    barrier = pltpu.get_barrier_semaphore()
    has_low, has_high = box > 0, box < runs - 1
    low, high = jnp.maximum(box - 1, 0), jnp.minimum(box + 1, runs - 1)
    mesh = pl.DeviceIdType.MESH
    if swaps:
        for d in range(1, n):
            peer = lax.rem(me + d, n)
            pl.semaphore_signal(barrier, 1, device_id={"samp": peer}, device_id_type=mesh)
    if halos:
        @pl.when(has_low)
        def _():
            pl.semaphore_signal(barrier, 1, device_id={"box": low}, device_id_type=mesh)

        @pl.when(has_high)
        def _():
            pl.semaphore_signal(barrier, 1, device_id={"box": high}, device_id_type=mesh)
    arrivals = n - 1 if swaps else 0
    if halos:
        arrivals = arrivals + has_low.astype(jnp.int32) + has_high.astype(jnp.int32)
    pl.semaphore_wait(barrier, arrivals)
    copies, locals_, ups, downs = [], [], [], []
    for j in range(halos):
        x, y = xs[swaps + j], ys[swaps + j]
        up = pltpu.make_async_remote_copy(
            x, y.at[0], halo_send.at[j, 0], halo_recv.at[j, 0],
            device_id={"box": high}, device_id_type=mesh)
        down = pltpu.make_async_remote_copy(
            x, y.at[2], halo_send.at[j, 1], halo_recv.at[j, 1],
            device_id={"box": low}, device_id_type=mesh)
        pl.when(has_high)(up.start)
        pl.when(has_low)(down.start)
        ups.append(up)
        downs.append(down)
    for d in [2, 1, 3] if n == 4 else range(1, n):
        for j in range(swaps):
            peer = lax.rem(me + d, n)
            copy = pltpu.make_async_remote_copy(
                xs[j].at[peer // shares[j]], ys[j].at[me], send.at[j, d], recv.at[j, d],
                device_id={"samp": peer}, device_id_type=mesh)
            copy.start()
            copies.append(copy)
    for j in range(count):
        if j < swaps:
            copy = pltpu.make_async_copy(xs[j].at[me // shares[j]], ys[j].at[me], own.at[j])
        else:
            copy = pltpu.make_async_copy(xs[j], ys[j].at[1], own.at[j])
        copy.start()
        locals_.append(copy)
    for copy in locals_ + copies:
        copy.wait()
    for up, down in zip(ups, downs):
        pl.when(has_high)(up.wait_send)
        pl.when(has_low)(down.wait_send)
        pl.when(has_low)(up.wait_recv)
        pl.when(has_high)(down.wait_recv)


def exchange(number, swaps, halos):
    n, runs = lax.axis_size("samp"), lax.axis_size("box")
    arrays = [x for x, _ in swaps] + list(halos)
    shapes = [jax.ShapeDtypeStruct((n,) + x.shape[1:], x.dtype) for x, _ in swaps]
    shapes += [jax.ShapeDtypeStruct((3,) + x.shape, x.dtype) for x in halos]
    dma = pltpu.SemaphoreType.DMA
    return pl.pallas_call(
        functools.partial(
            exchange_kernel, n, runs, len(swaps), len(halos), tuple(s for _, s in swaps)),
        in_specs=[pl.BlockSpec(memory_space=pl.ANY)] * len(arrays),
        out_specs=[pl.BlockSpec(memory_space=pl.ANY)] * len(arrays),
        out_shape=shapes,
        scratch_shapes=[
            dma((max(len(swaps), 1), n)),
            dma((max(len(swaps), 1), n)),
            dma((len(arrays),)),
            dma((max(len(halos), 1), 2)),
            dma((max(len(halos), 1), 2)),
        ],
        compiler_params=pltpu.CompilerParams(
            collective_id=number, has_side_effects=True, vmem_limit_bytes=VMEM_LIMIT),
    )(*arrays)


def ranks(key):
    count = key.shape[0]
    ids = jnp.arange(count, dtype=jnp.int32)
    before = (key[None, :] < key[:, None]) | (
        (key[None, :] == key[:, None]) & (ids[None, :] < ids[:, None]))
    rank = jnp.sum(before.astype(jnp.int32), axis=1)
    order = jnp.sum(jnp.where(rank[None, :] == ids[:, None], ids[None, :], 0), axis=1)
    return rank, order


def pick(values, index):
    hot = index[:, None] == jnp.arange(values.shape[0], dtype=jnp.int32)[None, :]
    return jnp.sum(jnp.where(hot, values[None, :], 0), axis=1)


def body(
    radiation, theta_mid, phi_mid, theta_top, phi_top, shift_mid, shift_top,
    octant_low, octant_mid, parent_low, parent_mid, trans_low, trans_mid, trans_top,
    far_low, far_mid, far_top, offset_low, offset_mid, offset_top,
):
    n = lax.axis_size("samp")
    me, box = lax.axis_index("samp"), lax.axis_index("box")
    lows, mids = octant_low.shape[0], octant_mid.shape[0]
    tops = mids // 4
    low_each, mid_each, share = lows // n, mids // n, n // tops
    _, _, rows_low, p_low = radiation.shape
    rank_mid, order_mid = ranks(parent_mid)
    rank_low, order_low = ranks(pick(rank_mid, parent_low - box * mids))
    oct_low = lax.dynamic_slice_in_dim(pick(octant_low, order_low), me * low_each, low_each)
    oct_mid = lax.dynamic_slice_in_dim(pick(octant_mid, order_mid), me * mid_each, mid_each)

    grouped = jnp.take(radiation, order_low, axis=1)
    grouped = jnp.moveaxis(grouped.reshape(2, n, low_each, rows_low, p_low), 1, 0)
    low_parts, near_low = exchange(0, [(grouped, 1)], [radiation])
    mid_parts = go_up(low_parts, theta_mid, phi_mid, shift_mid, oct_low, mid_each)
    mid_rows, = exchange(1, [(mid_parts, 1)], [])
    top_parts = go_up(mid_parts, theta_top, phi_top, shift_top, oct_mid, 1)
    middle = jnp.moveaxis(mid_rows, 0, 1).reshape(2, mids, *mid_rows.shape[3:])
    middle = jnp.take(middle, rank_mid, axis=1)
    top_rows, near_mid = exchange(2, [(top_parts, 1)], [middle])
    summit = top_rows.reshape(tops, share, 2, *top_rows.shape[3:]).sum(axis=1)
    summit = jnp.moveaxis(summit, 0, 1)
    near_top, = exchange(3, [], [summit])
    in_mid = translate(near_mid, trans_mid, far_mid[order_mid], offset_mid[order_mid], mid_each)
    in_top = translate(near_top, trans_top, far_top, offset_top, 1)
    top_here, mid_here = exchange(4, [(in_top, share), (in_mid, 1)], [])
    mid_in = go_down(top_here, theta_top, phi_top, shift_top, oct_mid, mid_here)
    low_in = go_down(mid_in, theta_mid, phi_mid, shift_mid, oct_low, None)
    low_rows, = exchange(5, [(low_in, 1)], [])
    out = translate(
        near_low, trans_low, far_low, offset_low, lows, low_rows, rank_low, low_each)
    return out.reshape(2, lows, rows_low, p_low)


def solution(mesh):
    in_specs = (
        P(None, "box", "samp", None),
        P(), P(), P(), P(), P(), P(),
        P("box"), P("box"), P("box"), P("box"),
        P(None, None, "samp", None),
        P(None, None, "samp", None),
        P(None, None, "samp", None),
        P("box", None), P("box", None), P("box", None),
        P("box", None), P("box", None), P("box", None),
    )
    out_specs = P(None, "box", "samp", None)
    return jax.shard_map(body, mesh=mesh, in_specs=in_specs, out_specs=out_specs, check_vma=False)
```

time: 986 us -> 211 us (0.21); the launches traced: 970 us -> 210 us
  local copies, waits for them, and re-layouts: 402 us -> 32.4 us
  other arithmetic: 352 us -> 5.7 us
  Pallas kernels: 0 us -> 172 us
  matrix products: 97.6 us -> 0 us
  waiting for transfers between devices: 84 us -> 0 us
  starting transfers between devices: 17.1 us -> 0 us
  between operations: 13.8 us -> 0.45 us
    gather x104 -> x4, local copies, waits for them, and re-layouts: 325 us -> 5.74 us  [the longest x1 3.08 us: body(): grouped = jnp.take(radiation, order_low, axis=1)]
    pallas_call x0 -> x13, Pallas kernels: none -> 172 us  [the longest x6 121 us: exchange(): pl.pallas_call(functools.partial(exchange_kernel, n, runs, len(swaps), le...]
    add x48 -> x4, other arithmetic: 149 us -> 0.07 us  [the longest x3 0.05 us: translate(): entry = local // boxes * (2 * boxes) + local % boxes]
    dot_general x12 -> x0, matrix products: 97.6 us -> none  [the longest x2 35.5 us: add_rows(): return jnp.einsum('st,rcsq->rctq', theta_cols, shifted, precision=highest)]
    all_gather x4 -> x0, waiting for transfers between devices: 83.9 us -> none  [the longest x2 83.9 us: aggregate(): lax.all_gather(interp, 'samp', axis=2, tiled=True)]
    select_n x146 -> x4, other arithmetic: 69.3 us -> 1.34 us  [the longest x2 1.34 us: body(): middle = jnp.take(middle, rank_mid, axis=1)]
    another operation x8 -> x0, other arithmetic: 64.5 us -> none  [shift_pattern(): return jnp.stack([real_part, imag_part])]
    sub x50 -> x1, other arithmetic: 47.5 us -> 0.66 us  [body(): rank_low, order_low = ranks(pick(rank_mid, parent_low - box * mids))]
  transfers between devices with their start and end apart: 10 -> 0, of which waited for: 1 -> 0; matrix products, arithmetic and copies ran while one was open for 51% -> 0% of each run, Pallas kernels for 0% -> 0%
where the time goes in v1:
time: 211 us; the launch traced here: 210 us
  Pallas kernels  172 us (82%)
  local copies, waits for them, and re-layouts  32.4 us (15%)
  other arithmetic  5.7 us (3%)
    pallas_call x6, Pallas kernels, exchange(): pl.pallas_call(functools.partial(exchange_kernel, n, runs, len(swaps), le...  121 us
    unnamed x63, local copies, waits for them, and re-layouts  24.8 us
    pallas_call x3, Pallas kernels, translate(): pl.pallas_call(functools.partial(translate_kernel, boxes, group, noff, ad...  21.6 us
    pallas_call x2, Pallas kernels, go_down(): pl.pallas_call(functools.partial(down_kernel, n, kids, with_add), grid_sp...  15.1 us
    pallas_call x2, Pallas kernels, go_up(): pl.pallas_call(functools.partial(up_kernel, n, kids), grid_spec=spec, out...  14.2 us

profile of v1, /device:TPU:8, one launch (start us, length us, event | category | flops | bytes accessed | tf_op | source)
XLA Modules:
  0.0 210.3 jit_solution(7134165885945608739)
XLA Ops:
  0.0 0.9 convert_reduce_fusion.1
  0.9 0.7 broadcast_subtract_fusion
  1.6 0.1 select_reduce_fusion.4
  1.7 0.2 convert_reduce_fusion
  1.8 0.1 select_reduce_fusion.1
  2.0 0.8 select_reduce_fusion
  2.8 0.1 dynamic_slice.6.oct_ref
  2.9 3.1 %gather_fusion = f32[32,2,22,168]{3,0,2,1:T(8,128)S(1)} fusion(f32[2,32,22,168]{3,1,2,0:T(8,128)} %param.20, s32[1024]{0:T(1024)S(1)} %pad_clamp_fusion.2), kind=kCustom, calls=%fused_computation | custom fusion | bytes 1892480 | tf_op jit(solution)/shard_map/jit(_take)/gather | solution.py:337
  6.0 0.0 copy-start.20
  6.0 0.1 reduce_sum.84
  6.1 0.9 fusion.refs_0_
  7.0 0.3 copy-done.20
  7.3 0.8 copy.60.refs_1_
  8.2 0.0 copy-start.1
  8.2 0.0 copy-start.13
  8.2 21.1 %shard_map.190 = (f32[4,2,8,22,168]{4,3,2,1,0:T(8,128)S(1)}, f32[3,2,32,22,168]{4,3,2,1,0:T(8,128)}) custom-call(f32[4,2,8,22,168]{4,3,2,1,0:T(8,128)S(1)} %fusion.refs_0_, f32[2,32,22,168]{3,2,1,0:T(8,128)S(1)} %copy.60.refs_1_), custom_call_target="tpu_custom_call" | custom-call | tf_op jit(solution)/shard_map/pallas_call | solution.py:288
  29.4 0.0 copy-start.26
  29.4 0.0 copy-start.4
  29.4 7.7 %shard_map.191.x_ref.refs_0_ = f32[4,2,2,40,312]{4,3,2,1,0:T(8,128)S(1)} custom-call(s32[8]{0:T(128)S(1)} %dynamic_slice.6.oct_ref, f32[4,2,8,22,168]{4,3,2,1,0:T(8,128)S(1)} %get-tuple-element.12.x_ref, f32[160,88]{1,0:T(8,128)S(1)} %copy-done.18, f32[168,312]{1,0:T(8,128)S(1)} %bitcast.51, f32[8,160,312]{2,1,0:T(8,128)S(1)} %copy-done.1), custom_call_target="tpu_custom_call" | custom-call | tf_op jit(solution)/shard_map/pallas_call | solution.py:91
  37.1 0.1 select_reduce_fusion.3
  37.2 0.2 select_reduce_fusion.2
  37.4 0.1 dynamic_slice.7.oct_ref
  37.5 1.8 copy.62.q_ref
  39.3 1.0 copy-done.12
  40.2 6.6 %shard_map.192.refs_0_ = f32[4,2,1,74,584]{4,3,2,1,0:T(8,128)S(1)} custom-call(s32[2]{0:T(128)S(1)} %dynamic_slice.7.oct_ref, f32[4,2,2,40,312]{4,3,2,1,0:T(8,128)S(1)} %shard_map.191.x_ref.refs_0_, f32[296,160]{1,0:T(8,128)S(1)} %copy-done.12, f32[312,584]{1,0:T(8,128)S(1)} %bitcast.46, f32[8,296,584]{2,1,0:T(8,128)} %shift_ref.6), custom_call_target="tpu_custom_call" | custom-call | tf_op jit(solution)/shard_map/pallas_call | solution.py:91
  46.8 14.7 %shard_map.193 = f32[4,2,2,40,312]{4,3,2,1,0:T(8,128)S(1)} custom-call(f32[4,2,2,40,312]{4,3,2,1,0:T(8,128)S(1)} %shard_map.191.x_ref.refs_0_), custom_call_target="tpu_custom_call" | custom-call | tf_op jit(solution)/shard_map/pallas_call | solution.py:288
  61.5 0.1 copy.63
  61.6 1.6 gather_fusion.1
  63.1 1.3 fusion.1.refs_1_
  64.5 21.3 %shard_map.194 = (f32[4,2,1,74,584]{4,3,2,1,0:T(8,128)S(1)}, f32[3,2,8,40,312]{4,3,2,1,0:T(8,128)}) custom-call(f32[4,2,1,74,584]{4,3,2,1,0:T(8,128)S(1)} %shard_map.192.refs_0_, f32[2,8,40,312]{3,2,1,0:T(8,128)S(1)} %fusion.1.refs_1_), custom_call_target="tpu_custom_call" | custom-call | tf_op jit(solution)/shard_map/pallas_call | solution.py:288
  85.9 1.2 copy-done.8
  87.0 0.6 gather_fusion.2
  87.6 0.6 gather_fusion.3
  88.2 1.8 copy-done.6
  90.0 1.5 copy-done.7
  91.6 5.4 %shard_map.197 = f32[16,40,312]{2,1,0:T(8,128)S(1)} custom-call(s32[8,16]{1,0:T(8,128)S(1)} %fusion.11.e_ref, s32[8,16]{1,0:T(8,128)S(1)} %gather_fusion.3, f32[48,40,312]{2,1,0:T(8,128)S(1)} %bitcast.48, f32[32,40,312]{2,1,0:T(8,128)S(1)} %bitcast.49), custom_call_target="tpu_custom_call" | custom-call | tf_op jit(solution)/shard_map/pallas_call | solution.py:209
  97.0 0.2 reduce_sum.90
  97.2 0.1 copy.79
  97.3 11.9 %shard_map.195 = f32[3,2,2,74,584]{4,3,2,1,0:T(8,128)S(1)} custom-call(f32[2,2,74,584]{3,2,1,0:T(8,128)S(1)} %bitcast.44), custom_call_target="tpu_custom_call" | custom-call | tf_op jit(solution)/shard_map/pallas_call | solution.py:288
  109.3 0.0 copy-start.19
  109.3 7.3 %copy.66 = f32[2,16,74,584]{3,2,1,0:T(8,128)} copy(f32[2,16,74,584]{3,1,2,0:T(8,128)} %param.33) | data formatting | bytes 11063296 | tf_op args[13]
  116.6 6.7 %shard_map.196 = f32[4,74,584]{2,1,0:T(8,128)S(1)} custom-call(s32[2,16]{1,0:T(2,128)S(1)} %fusion.18.e_ref, s32[2,16]{1,0:T(2,128)S(1)} %copy-done.19, f32[12,74,584]{2,1,0:T(8,128)S(1)} %bitcast.39, f32[32,74,584]{2,1,0:T(8,128)} %bitcast.54), custom_call_target="tpu_custom_call" | custom-call | tf_op jit(solution)/shard_map/pallas_call | solution.py:209
  123.2 0.0 copy-start.5
  123.3 31.7 %shard_map.198 = (f32[4,2,1,74,584]{4,3,2,1,0:T(8,128)S(1)}, f32[4,2,2,40,312]{4,3,2,1,0:T(8,128)S(1)}) custom-call(f32[2,2,1,74,584]{4,3,2,1,0:T(8,128)S(1)} %bitcast.45, f32[4,2,2,40,312]{4,3,2,1,0:T(8,128)S(1)} %bitcast.42), custom_call_target="tpu_custom_call" | custom-call | tf_op jit(solution)/shard_map/pallas_call | solution.py:288
  154.9 1.2 copy-done.10
  156.1 0.9 copy-done.15
  157.1 1.2 copy.67.r_ref
  158.3 1.2 copy-done.3
  159.5 1.4 copy-done.11
  160.9 1.2 copy-done.16
  162.1 7.1 %shard_map.199.g_ref = f32[4,2,2,40,312]{4,3,2,1,0:T(8,128)S(1)} custom-call(s32[2]{0:T(128)S(1)} %dynamic_slice.7.oct_ref, f32[4,2,1,74,584]{4,3,2,1,0:T(8,128)S(1)} %copy-done.11, f32[160,296]{1,0:T(8,128)S(1)} %bitcast.52, f32[584,312]{1,0:T(8,128)S(1)} %copy-done.3, f32[8,296,584]{2,1,0:T(8,128)} %shift_ref.6, f32[4,2,2,40,312]{4,3,2,1,0:T(8,128)S(1)} %copy-done.16), custom_call_target="tpu_custom_call" | custom-call | tf_op jit(solution)/shard_map/pallas_call | solution.py:152
  169.2 0.1 copy.69.r_ref
  169.4 1.0 copy.68
  170.4 7.9 %shard_map.200.refs_0_ = f32[4,2,8,22,168]{4,3,2,1,0:T(8,128)S(1)} custom-call(s32[8]{0:T(128)S(1)} %dynamic_slice.6.oct_ref, f32[4,2,2,40,312]{4,3,2,1,0:T(8,128)S(1)} %shard_map.199.g_ref, f32[88,160]{1,0:T(8,128)S(1)} %bitcast.53, f32[312,168]{1,0:T(8,128)S(1)} %copy.69.r_ref, f32[8,160,312]{2,1,0:T(8,128)S(1)} %copy-done.2), custom_call_target="tpu_custom_call" | custom-call | tf_op jit(solution)/shard_map/pallas_call | solution.py:152
  178.3 0.0 copy-start.23
  178.4 0.0 copy-start.21
  178.4 20.1 %shard_map.201 = f32[4,2,8,22,168]{4,3,2,1,0:T(8,128)S(1)} custom-call(f32[4,2,8,22,168]{4,3,2,1,0:T(8,128)S(1)} %shard_map.200.refs_0_), custom_call_target="tpu_custom_call" | custom-call | tf_op jit(solution)/shard_map/pallas_call | solution.py:288
  198.5 0.0 copy-start.24
  198.6 0.1 copy.58
  198.7 0.4 copy.61
  199.1 0.1 copy-done.24
  199.2 0.1 copy.70.o_ref
  199.3 9.4 %shard_map.202 = f32[64,22,168]{2,1,0:T(8,128)S(1)} custom-call(s32[32,16]{1,0:T(8,128)S(1)} %fusion.3.e_ref, s32[32,16]{1,0:T(8,128)S(1)} %copy.70.o_ref, s32[32]{0:T(128)S(1)} %fusion.19.rest_0_, f32[192,22,168]{2,1,0:T(8,128)} %bitcast.56, f32[32,22,168]{2,1,0:T(8,128)S(1)} %bitcast.47, f32[64,22,168]{2,1,0:T(8,128)S(1)} %bitcast.40), custom_call_target="tpu_custom_call" | custom-call | tf_op jit(solution)/shard_map/pallas_call | solution.py:209
  208.7 1.5 copy.71
  (45 shorter events, 0.2 us)
Async XLA Ops:
  0.0 87.0 %copy-start = (s32[8,16]{1,0:T(8,128)S(1)}, s32[8,16]{1,0:T(8,128)}, u32[]{:S(2)}) copy-start(s32[8,16]{1,0:T(8,128)} %param.35) | copy-start | bytes 1540
  6.0 1.4 copy-start.20
  8.2 21.2 %copy-start.1 = (f32[8,160,312]{2,1,0:T(8,128)S(1)}, f32[8,160,312]{2,1,0:T(8,128)}, u32[]{:S(2)}) copy-start(f32[8,160,312]{2,1,0:T(8,128)} %shift_ref.7) | copy-start | bytes 4792324
  8.2 21.2 %copy-start.13 = (f32[312,168]{0,1:T(8,128)S(1)}, f32[312,168]{0,1:T(8,128)}, u32[]{:S(2)}) copy-start(f32[312,168]{0,1:T(8,128)} %param.22) | copy-start | bytes 628996
  8.2 21.2 %copy-start.18 = (f32[160,88]{1,0:T(8,128)S(1)}, f32[160,88]{1,0:T(8,128)}, u32[]{:S(2)}) copy-start(f32[160,88]{1,0:T(8,128)} %q_ref.2) | copy-start | bytes 168964
  29.4 7.8 %copy-start.26 = (s32[8]{0:T(128)S(1)}, s32[8]{0:T(128)}, u32[]{:S(2)}) copy-start(s32[8]{0:T(128)} %param.28) | copy-start | bytes 100
  29.4 9.9 %copy-start.4 = (f32[584,312]{0,1:T(8,128)S(1)}, f32[584,312]{0,1:T(8,128)}, u32[]{:S(2)}) copy-start(f32[584,312]{0,1:T(8,128)} %param.24) | copy-start | bytes 2186500
  39.3 1.0 copy-start.12
  64.5 23.1 %copy-start.22 = (s32[8,16]{1,0:T(8,128)S(1)}, s32[8,16]{1,0:T(8,128)}, u32[]{:S(2)}) copy-start(s32[8,16]{1,0:T(8,128)} %param.38) | copy-start | bytes 1540
  85.8 1.2 copy-start.8
  88.2 1.8 copy-start.6
  90.0 1.5 copy-start.7
  91.6 5.4 %copy-start.9 = (f32[4,2,1,74,584]{4,3,2,1,0:T(8,128)S(1)}, f32[4,2,1,74,584]{4,3,2,1,0:T(8,128)}, u32[]{:S(2)}) copy-start(f32[4,2,1,74,584]{4,3,2,1,0:T(8,128)} %copy-done.8) | copy-start | bytes 4148740
  97.3 11.9 %copy-start.25 = (s32[2,16]{1,0:T(2,128)S(1)}, s32[2,16]{1,0:T(2,128)}, u32[]{:S(2)}) copy-start(s32[2,16]{1,0:T(2,128)} %param.36) | copy-start | bytes 388
  109.3 7.3 %copy-start.19 = (s32[2,16]{1,0:T(2,128)S(1)}, s32[2,16]{1,0:T(2,128)}, u32[]{:S(2)}) copy-start(s32[2,16]{1,0:T(2,128)} %o_ref.2) | copy-start | bytes 388
  123.2 33.8 %copy-start.5 = (f32[584,312]{0,1:T(8,128)S(1)}, f32[584,312]{0,1:T(8,128)}, u32[]{:S(2)}) copy-start(f32[584,312]{0,1:T(8,128)} %param.24) | copy-start | bytes 2186500
  123.3 35.1 %copy-start.17 = (f32[296,160]{0,1:T(8,128)S(1)}, f32[296,160]{0,1:T(8,128)}, u32[]{:S(2)}) copy-start(f32[296,160]{0,1:T(8,128)} %param.23) | copy-start | bytes 568324
  154.9 1.2 copy-start.10
  156.1 0.9 copy-start.15
  158.3 1.2 copy-start.3
  159.5 1.4 copy-start.11
  160.9 1.2 copy-start.16
  162.1 7.1 %copy-start.14 = (f32[312,168]{0,1:T(8,128)S(1)}, f32[312,168]{0,1:T(8,128)}, u32[]{:S(2)}) copy-start(f32[312,168]{0,1:T(8,128)} %param.22) | copy-start | bytes 628996
  162.1 8.3 %copy-start.2 = (f32[8,160,312]{2,1,0:T(8,128)S(1)}, f32[8,160,312]{2,1,0:T(8,128)}, u32[]{:S(2)}) copy-start(f32[8,160,312]{2,1,0:T(8,128)} %shift_ref.7) | copy-start | bytes 4792324
  178.3 20.2 %copy-start.23 = (s32[32,16]{0,1:T(8,128)S(1)}, s32[32,16]{0,1:T(8,128)}, u32[]{:S(2)}) copy-start(s32[32,16]{0,1:T(8,128)} %param.34) | copy-start | bytes 6148
  178.4 20.3 %copy-start.21 = (f32[2,16,22,168]{3,1,2,0:T(8,128)S(1)}, f32[2,16,22,168]{3,1,2,0:T(8,128)}, u32[]{:S(2)}) copy-start(f32[2,16,22,168]{3,1,2,0:T(8,128)} %param.31) | copy-start | bytes 1419268
  198.5 0.7 copy-start.24

commit v2 on v1

--- a/solution.py
+++ b/solution.py
@@ -157,63 +157,247 @@
     )(*args)
 
 
-def translate_kernel(boxes, group, noff, with_add, chunk, e_ref, o_ref, *rest):
-    if with_add:
-        a_ref, pat, tab, add_ref, out_ref = rest
-    else:
-        pat, tab, out_ref = rest
+def sum_far(boxes, noff, chunk, b, e_ref, o_ref, pat, tab, store):
     rows = pat.shape[1]
-    far = e_ref.shape[1]
-
-    def step(b, carry):
-        place = (b // group) * (2 * group) + lax.rem(b, group)
-        for lo in range(0, rows, chunk):
-            here = slice(lo, min(lo + chunk, rows))
-            if with_add:
-                start = a_ref[b]
-                real = add_ref[start, here, :]
-                imag = add_ref[start + with_add, here, :]
-            else:
-                real = imag = None
-            for f in range(far):
-                e, o = e_ref[b, f], o_ref[b, f]
-                sr, si = pat[e, here, :], pat[e + boxes, here, :]
-                cr, ci = tab[o, here, :], tab[o + noff, here, :]
-                dr, di = sr * cr - si * ci, sr * ci + si * cr
-                real = dr if real is None else real + dr
-                imag = di if imag is None else imag + di
-            out_ref[place, here, :] = real
-            out_ref[place + group, here, :] = imag
+    for lo in range(0, rows, chunk):
+        here = slice(lo, min(lo + chunk, rows))
+        real = imag = None
+        for f in range(e_ref.shape[1]):
+            e, o = e_ref[b, f], o_ref[b, f]
+            sr, si = pat[e, here, :], pat[e + boxes, here, :]
+            cr, ci = tab[o, here, :], tab[o + noff, here, :]
+            dr, di = sr * cr - si * ci, sr * ci + si * cr
+            real = dr if real is None else real + dr
+            imag = di if imag is None else imag + di
+        store(here, real, imag)
+
+
+def chunk_of(p):
+    return 24 if p <= 256 else 16 if p <= 384 else 8
+
+
+def entries(far_ids, boxes):
+    local = far_ids - (lax.axis_index("box") - 1) * boxes
+    return (local // boxes) * (2 * boxes) + local % boxes
+
+
+MESH = pl.DeviceIdType.MESH
+
+
+def peers_of(n):
+    me = lax.axis_index("samp")
+    return [(d, lax.rem(me + d, n)) for d in ([2, 1, 3] if n == 4 else range(1, n))]
+
+
+def greet(n, runs, halos):
+    barrier = pltpu.get_barrier_semaphore()
+    for _, peer in peers_of(n):
+        pl.semaphore_signal(barrier, 1, device_id={"samp": peer}, device_id_type=MESH)
+    arrivals = n - 1
+    if halos:
+        box = lax.axis_index("box")
+        has_low, has_high = box > 0, box < runs - 1
+
+        @pl.when(has_low)
+        def _():
+            pl.semaphore_signal(barrier, 1, device_id={"box": box - 1}, device_id_type=MESH)
+
+        @pl.when(has_high)
+        def _():
+            pl.semaphore_signal(barrier, 1, device_id={"box": box + 1}, device_id_type=MESH)
+
+        arrivals = arrivals + has_low.astype(jnp.int32) + has_high.astype(jnp.int32)
+    pl.semaphore_wait(barrier, arrivals)
+
+
+def halo_copies(runs, near, size, send, recv):
+    box = lax.axis_index("box")
+    has_low, has_high = box > 0, box < runs - 1
+    own = near.at[pl.ds(size, size)]
+    up = pltpu.make_async_remote_copy(
+        own, near.at[pl.ds(0, size)], send.at[0], recv.at[0],
+        device_id={"box": jnp.minimum(box + 1, runs - 1)}, device_id_type=MESH)
+    down = pltpu.make_async_remote_copy(
+        own, near.at[pl.ds(2 * size, size)], send.at[1], recv.at[1],
+        device_id={"box": jnp.maximum(box - 1, 0)}, device_id_type=MESH)
+
+    def start():
+        pl.when(has_high)(up.start)
+        pl.when(has_low)(down.start)
+
+    def arrive():
+        pl.when(has_low)(up.wait_recv)
+        pl.when(has_high)(down.wait_recv)
+
+    def leave():
+        pl.when(has_high)(up.wait_send)
+        pl.when(has_low)(down.wait_send)
+
+    return start, arrive, leave
+
+
+def middle_kernel(
+    n, runs, e_mid, o_mid, rank, e_top, o_top, top_parts, mid_rows, tab_mid, tab_top,
+    top_here, mid_here, near_mid, near_top, top_rows, in_mid, in_top,
+    send, recv, halo_send, halo_recv,
+):
+    me = lax.axis_index("samp")
+    mids, tops = e_mid.shape[0], e_top.shape[0]
+    each, share = mids // n, n // tops
+    noff = tab_mid.shape[0] // 2
+    greet(n, runs, True)
+
+    def swap(j, src, dst, share):
+        copies = [
+            pltpu.make_async_remote_copy(
+                src.at[peer // share], dst.at[me], send.at[j, d], recv.at[j, d],
+                device_id={"samp": peer}, device_id_type=MESH)
+            for d, peer in peers_of(n)
+        ]
+        for copy in copies:
+            copy.start()
+        return copies
+
+    tops_out = swap(0, top_parts, top_rows, 1)
+
+    def natural(b, carry):
+        place = rank[b]
+        for r in range(2):
+            near_mid[(2 + r) * mids + b] = mid_rows[place // each, r, lax.rem(place, each)]
         return carry
 
-    lax.fori_loop(0, boxes, step, 0)
-
-
-def translate(near, table, far_ids, offsets, group, add=None, add_at=None, add_group=0):
-    _, _, boxes, rows, p = near.shape
-    noff = table.shape[1]
-    chunk = 24 if p <= 256 else 16 if p <= 384 else 8
-    first = (lax.axis_index("box") - 1) * boxes
-    local = far_ids - first
-    entry = (local // boxes) * (2 * boxes) + local % boxes
-    args = [entry, offsets]
-    specs = [pl.BlockSpec(memory_space=SMEM)] * 2
-    if add is not None:
-        args.append((add_at // add_group) * (2 * add_group) + add_at % add_group)
-        specs.append(pl.BlockSpec(memory_space=SMEM))
-    args += [near.reshape(6 * boxes, rows, p), table.reshape(2 * noff, rows, p)]
-    specs += [pl.BlockSpec(memory_space=VMEM)] * 2
-    if add is not None:
-        args.append(add.reshape(-1, rows, p))
-        specs.append(pl.BlockSpec(memory_space=VMEM))
-    out = pl.pallas_call(
-        functools.partial(translate_kernel, boxes, group, noff, add_group, chunk),
-        in_specs=specs,
-        out_specs=pl.BlockSpec(memory_space=VMEM),
-        out_shape=jax.ShapeDtypeStruct((2 * boxes, rows, p), jnp.float32),
-        compiler_params=pltpu.CompilerParams(vmem_limit_bytes=VMEM_LIMIT),
-    )(*args)
-    return out.reshape(boxes // group, 2, group, rows, p)
+    lax.fori_loop(0, mids, natural, 0)
+    start_mid, mid_arrives, mid_leaves = halo_copies(
+        runs, near_mid, 2 * mids, halo_send.at[0], halo_recv.at[0])
+    start_mid()
+    top_rows[me] = top_parts[me]
+    mid_arrives()
+
+    def far_mid(b, carry):
+        def store(here, real, imag):
+            in_mid[b // each, 0, lax.rem(b, each), here, :] = real
+            in_mid[b // each, 1, lax.rem(b, each), here, :] = imag
+
+        sum_far(mids, noff, chunk_of(tab_mid.shape[2]), b, e_mid, o_mid, near_mid, tab_mid, store)
+        return carry
+
+    lax.fori_loop(0, mids, far_mid, 0)
+    for copy in tops_out:
+        copy.wait()
+    mids_out = swap(1, in_mid, mid_here, 1)
+    mid_here[me] = in_mid[me]
+    for t in range(tops):
+        for r in range(2):
+            total = top_rows[t * share, r, 0]
+            for k in range(1, share):
+                total = total + top_rows[t * share + k, r, 0]
+            near_top[(2 + r) * tops + t] = total
+    start_top, top_arrives, top_leaves = halo_copies(
+        runs, near_top, 2 * tops, halo_send.at[1], halo_recv.at[1])
+    start_top()
+    top_arrives()
+
+    def far_top(b, carry):
+        def store(here, real, imag):
+            in_top[b, 0, 0, here, :] = real
+            in_top[b, 1, 0, here, :] = imag
+
+        sum_far(tops, noff, chunk_of(tab_top.shape[2]), b, e_top, o_top, near_top, tab_top, store)
+        return carry
+
+    lax.fori_loop(0, tops, far_top, 0)
+    tops_back = swap(2, in_top, top_here, share)
+    top_here[me] = in_top[me // share]
+    for copy in mids_out + tops_back:
+        copy.wait()
+    mid_leaves()
+    top_leaves()
+
+
+def flat(x, lead):
+    return x.reshape((-1,) + x.shape[lead:])
+
+
+def middle_stage(number, mid_rows, top_parts, rank, trans_mid, trans_top, e_mid, o_mid, e_top, o_top):
+    n, runs = lax.axis_size("samp"), lax.axis_size("box")
+    mids, tops = e_mid.shape[0], e_top.shape[0]
+    f32, dma = jnp.float32, pltpu.SemaphoreType.DMA
+    row_mid, row_top = mid_rows.shape[3:], top_parts.shape[3:]
+    spec = pl.BlockSpec(memory_space=VMEM)
+    return pl.pallas_call(
+        functools.partial(middle_kernel, n, runs),
+        in_specs=[pl.BlockSpec(memory_space=SMEM)] * 5 + [spec] * 4,
+        out_specs=[spec, spec],
+        out_shape=[
+            jax.ShapeDtypeStruct(top_parts.shape, f32),
+            jax.ShapeDtypeStruct(mid_rows.shape, f32),
+        ],
+        scratch_shapes=[
+            pltpu.VMEM((6 * mids,) + row_mid, f32),
+            pltpu.VMEM((6 * tops,) + row_top, f32),
+            pltpu.VMEM(top_parts.shape, f32),
+            pltpu.VMEM(mid_rows.shape, f32),
+            pltpu.VMEM((tops, 2, 1) + row_top, f32),
+            dma((3, n)), dma((3, n)), dma((2, 2)), dma((2, 2)),
+        ],
+        compiler_params=pltpu.CompilerParams(
+            collective_id=number, has_side_effects=True, vmem_limit_bytes=VMEM_LIMIT),
+    )(e_mid, o_mid, rank, e_top, o_top, top_parts, mid_rows, flat(trans_mid, 2), flat(trans_top, 2))
+
+
+def last_kernel(n, runs, e_ref, o_ref, at_ref, low_in, pat, tab, out_ref, landed, send, recv):
+    me = lax.axis_index("samp")
+    boxes = e_ref.shape[0]
+    size = low_in.shape[0] // n
+    noff = tab.shape[0] // 2
+    greet(n, runs, False)
+    copies = [
+        pltpu.make_async_remote_copy(
+            low_in.at[pl.ds(peer * size, size)], landed.at[pl.ds(me * size, size)],
+            send.at[d], recv.at[d], device_id={"samp": peer}, device_id_type=MESH)
+        for d, peer in peers_of(n)
+    ]
+    for copy in copies:
+        copy.start()
+    landed[pl.ds(me * size, size)] = low_in[pl.ds(me * size, size)]
+
+    def far(b, carry):
+        def store(here, real, imag):
+            out_ref[b, here, :] = real
+            out_ref[b + boxes, here, :] = imag
+
+        sum_far(boxes, noff, chunk_of(tab.shape[2]), b, e_ref, o_ref, pat, tab, store)
+        return carry
+
+    lax.fori_loop(0, boxes, far, 0)
+    for copy in copies:
+        copy.wait()
+
+    def add(b, carry):
+        place = at_ref[b]
+        out_ref[b] = out_ref[b] + landed[place]
+        out_ref[b + boxes] = out_ref[b + boxes] + landed[place + size // 2]
+        return carry
+
+    lax.fori_loop(0, boxes, add, 0)
+
+
+def last_stage(number, low_in, near, table, e_low, o_low, rank):
+    n, runs = lax.axis_size("samp"), lax.axis_size("box")
+    boxes, each = e_low.shape[0], low_in.shape[2]
+    row = low_in.shape[3:]
+    place = (rank // each) * (2 * each) + rank % each
+    dma = pltpu.SemaphoreType.DMA
+    spec = pl.BlockSpec(memory_space=VMEM)
+    return pl.pallas_call(
+        functools.partial(last_kernel, n, runs),
+        in_specs=[pl.BlockSpec(memory_space=SMEM)] * 3 + [spec] * 3,
+        out_specs=spec,
+        out_shape=jax.ShapeDtypeStruct((2 * boxes,) + row, jnp.float32),
+        scratch_shapes=[pltpu.VMEM((2 * boxes,) + row, jnp.float32), dma((n,)), dma((n,))],
+        compiler_params=pltpu.CompilerParams(
+            collective_id=number, has_side_effects=True, vmem_limit_bytes=VMEM_LIMIT),
+    )(e_low, o_low, place, flat(low_in, 3), flat(near, 3), flat(table, 2)).reshape((2, boxes) + row)
 
 
 def exchange_kernel(n, runs, swaps, halos, shares, *refs):
@@ -327,7 +511,7 @@
     me, box = lax.axis_index("samp"), lax.axis_index("box")
     lows, mids = octant_low.shape[0], octant_mid.shape[0]
     tops = mids // 4
-    low_each, mid_each, share = lows // n, mids // n, n // tops
+    low_each, mid_each = lows // n, mids // n
     _, _, rows_low, p_low = radiation.shape
     rank_mid, order_mid = ranks(parent_mid)
     rank_low, order_low = ranks(pick(rank_mid, parent_low - box * mids))
@@ -340,21 +524,14 @@
     mid_parts = go_up(low_parts, theta_mid, phi_mid, shift_mid, oct_low, mid_each)
     mid_rows, = exchange(1, [(mid_parts, 1)], [])
     top_parts = go_up(mid_parts, theta_top, phi_top, shift_top, oct_mid, 1)
-    middle = jnp.moveaxis(mid_rows, 0, 1).reshape(2, mids, *mid_rows.shape[3:])
-    middle = jnp.take(middle, rank_mid, axis=1)
-    top_rows, near_mid = exchange(2, [(top_parts, 1)], [middle])
-    summit = top_rows.reshape(tops, share, 2, *top_rows.shape[3:]).sum(axis=1)
-    summit = jnp.moveaxis(summit, 0, 1)
-    near_top, = exchange(3, [], [summit])
-    in_mid = translate(near_mid, trans_mid, far_mid[order_mid], offset_mid[order_mid], mid_each)
-    in_top = translate(near_top, trans_top, far_top, offset_top, 1)
-    top_here, mid_here = exchange(4, [(in_top, share), (in_mid, 1)], [])
+    top_here, mid_here = middle_stage(
+        2, mid_rows, top_parts, rank_mid, trans_mid, trans_top,
+        entries(far_mid, mids)[order_mid], offset_mid[order_mid],
+        entries(far_top, tops), offset_top)
     mid_in = go_down(top_here, theta_top, phi_top, shift_top, oct_mid, mid_here)
     low_in = go_down(mid_in, theta_mid, phi_mid, shift_mid, oct_low, None)
-    low_rows, = exchange(5, [(low_in, 1)], [])
-    out = translate(
-        near_low, trans_low, far_low, offset_low, lows, low_rows, rank_low, low_each)
-    return out.reshape(2, lows, rows_low, p_low)
+    return last_stage(
+        3, low_in, near_low, trans_low, entries(far_low, lows), offset_low, rank_low)
 
 
 def solution(mesh):

time: 211 us -> 183 us (0.87)
  Pallas kernels: 172 us -> 147 us
  local copies, waits for them, and re-layouts: 32.4 us -> 30.2 us
    pallas_call x6 -> x2, Pallas kernels: 121 us -> 35.8 us  [exchange(): pl.pallas_call(functools.partial(exchange_kernel, n, runs, len(swaps), le...]
    pallas_call x3 -> x2, Pallas kernels: 21.6 us -> 82.3 us  [the longest x1 58.5 us: middle_stage(): pl.pallas_call(functools.partial(middle_kernel, n, runs), in_specs=[pl.Bl...]
    unnamed x63 -> x59, local copies, waits for them, and re-layouts: 24.8 us -> 24.2 us
where the time goes in v2:
time: 183 us; the launch traced here: 182 us
  Pallas kernels  147 us (80%)
  local copies, waits for them, and re-layouts  30.2 us (17%)
  other arithmetic  4.15 us (2%)
    pallas_call x1, Pallas kernels, middle_stage(): pl.pallas_call(functools.partial(middle_kernel, n, runs), in_specs=[pl.Bl...  58.5 us
    pallas_call x2, Pallas kernels, exchange(): pl.pallas_call(functools.partial(exchange_kernel, n, runs, len(swaps), le...  35.8 us
    unnamed x59, local copies, waits for them, and re-layouts  24.2 us
    pallas_call x1, Pallas kernels, last_stage(): pl.pallas_call(functools.partial(last_kernel, n, runs), in_specs=[pl.Bloc...  23.9 us
    pallas_call x2, Pallas kernels, go_down(): pl.pallas_call(functools.partial(down_kernel, n, kids, with_add), grid_sp...  14.9 us
    pallas_call x2, Pallas kernels, go_up(): pl.pallas_call(functools.partial(up_kernel, n, kids), grid_spec=spec, out...  14.2 us

profile of v2, /device:TPU:8, one launch (start us, length us, event | category | flops | bytes accessed | tf_op | source)
XLA Modules:
  0.0 181.9 jit_solution(17795743696351591215)
XLA Ops:
  0.0 0.0 copy-start
  0.0 0.7 broadcast_subtract_fusion
  0.7 0.9 convert_reduce_fusion.1.rank
  1.6 0.1 select_reduce_fusion.4
  1.7 0.2 convert_reduce_fusion
  1.9 0.1 select_reduce_fusion.1
  2.0 0.8 select_reduce_fusion
  2.8 0.1 dynamic_slice.6.oct_ref
  2.9 3.1 %gather_fusion.2 = f32[32,2,22,168]{3,0,2,1:T(8,128)S(1)} fusion(f32[2,32,22,168]{3,1,2,0:T(8,128)} %param.20, s32[1024]{0:T(1024)S(1)} %pad_clamp_fusion), kind=kCustom, calls=%fused_computation.2 | custom fusion | bytes 1892480 | tf_op jit(solution)/shard_map/jit(_take)/gather | solution.py:521
  6.0 0.0 copy-start.19
  6.0 0.1 reduce_sum.77
  6.1 0.9 fusion.refs_0_
  7.1 0.3 copy-done.19
  7.4 0.8 copy.44.refs_1_
  8.2 0.0 copy-start.1
  8.2 0.0 copy-start.13
  8.2 0.0 copy-start.17
  8.2 21.1 %shard_map.190 = (f32[4,2,8,22,168]{4,3,2,1,0:T(8,128)S(1)}, f32[3,2,32,22,168]{4,3,2,1,0:T(8,128)}) custom-call(f32[4,2,8,22,168]{4,3,2,1,0:T(8,128)S(1)} %fusion.refs_0_, f32[2,32,22,168]{3,2,1,0:T(8,128)S(1)} %copy.44.refs_1_), custom_call_target="tpu_custom_call" | custom-call | tf_op jit(solution)/shard_map/pallas_call | solution.py:472
  29.4 0.0 copy-done.1
  29.4 0.0 copy-done.13
  29.4 0.0 copy-done.17
  29.4 0.0 copy-start.24
  29.4 7.7 %shard_map.191.x_ref.refs_0_ = f32[4,2,2,40,312]{4,3,2,1,0:T(8,128)S(1)} custom-call(s32[8]{0:T(128)S(1)} %dynamic_slice.6.oct_ref, f32[4,2,8,22,168]{4,3,2,1,0:T(8,128)S(1)} %get-tuple-element.9.x_ref, f32[160,88]{1,0:T(8,128)S(1)} %copy-done.17, f32[168,312]{1,0:T(8,128)S(1)} %bitcast.27, f32[8,160,312]{2,1,0:T(8,128)S(1)} %copy-done.1), custom_call_target="tpu_custom_call" | custom-call | tf_op jit(solution)/shard_map/pallas_call | solution.py:91
  37.1 0.1 select_reduce_fusion.3
  37.2 0.0 copy-done.24
  37.2 0.2 select_reduce_fusion.2
  37.4 0.1 dynamic_slice.7.oct_ref
  37.5 1.1 copy.45.q_ref
  38.5 0.0 copy-start.9
  38.6 1.1 copy-done.9
  39.7 6.6 %shard_map.192.top_parts = f32[4,2,1,74,584]{4,3,2,1,0:T(8,128)S(1)} custom-call(s32[2]{0:T(128)S(1)} %dynamic_slice.7.oct_ref, f32[4,2,2,40,312]{4,3,2,1,0:T(8,128)S(1)} %shard_map.191.x_ref.refs_0_, f32[296,160]{1,0:T(8,128)S(1)} %copy.45.q_ref, f32[312,584]{1,0:T(8,128)S(1)} %bitcast.25, f32[8,296,584]{2,1,0:T(8,128)} %shift_ref.6), custom_call_target="tpu_custom_call" | custom-call | tf_op jit(solution)/shard_map/pallas_call | solution.py:91
  46.3 1.2 copy-done.2
  47.5 14.6 %shard_map.193.mid_rows = f32[4,2,2,40,312]{4,3,2,1,0:T(8,128)S(1)} custom-call(f32[4,2,2,40,312]{4,3,2,1,0:T(8,128)S(1)} %shard_map.191.x_ref.refs_0_), custom_call_target="tpu_custom_call" | custom-call | tf_op jit(solution)/shard_map/pallas_call | solution.py:472
  62.1 0.0 copy-start.6
  62.1 0.9 copy-done.6
  63.1 0.6 gather_fusion
  63.7 0.6 gather_fusion.1
  64.3 0.0 copy-start.7
  64.3 0.0 copy-start.18
  64.3 7.4 %copy.46 = f32[2,16,74,584]{3,2,1,0:T(8,128)} copy(f32[2,16,74,584]{3,1,2,0:T(8,128)} %param.33) | data formatting | bytes 11063296 | tf_op args[13]
  71.7 0.0 copy-done.18
  71.7 0.0 copy-start.10
  71.8 58.5 %shard_map.194 = (f32[4,2,1,74,584]{4,3,2,1,0:T(8,128)S(1)}, f32[4,2,2,40,312]{4,3,2,1,0:T(8,128)S(1)}) custom-call(s32[8,16]{1,0:T(8,128)S(1)} %gather_fusion, s32[8,16]{1,0:T(8,128)S(1)} %gather_fusion.1, s32[8]{0:T(128)S(1)} %convert_reduce_fusion.1.rank, s32[2,16]{1,0:T(2,128)S(1)} %fusion.17.e_top, s32[2,16]{1,0:T(2,128)S(1)} %copy-done.18, ...), custom_call_target="tpu_custom_call" | custom-call | tf_op jit(solution)/shard_map/pallas_call | solution.py:327
  130.2 1.2 copy-done.11
  131.4 0.9 copy-done.14
  132.3 0.0 copy-done.10
  132.3 1.2 copy.47.r_ref
  133.6 0.0 copy-done.16
  133.6 1.2 copy-done.8
  134.8 1.4 copy-done.12
  136.2 1.2 copy-done.15
  137.4 7.0 %shard_map.195.g_ref = f32[4,2,2,40,312]{4,3,2,1,0:T(8,128)S(1)} custom-call(s32[2]{0:T(128)S(1)} %dynamic_slice.7.oct_ref, f32[4,2,1,74,584]{4,3,2,1,0:T(8,128)S(1)} %copy-done.12, f32[160,296]{1,0:T(8,128)S(1)} %bitcast.28, f32[584,312]{1,0:T(8,128)S(1)} %copy-done.8, f32[8,296,584]{2,1,0:T(8,128)} %shift_ref.6, f32[4,2,2,40,312]{4,3,2,1,0:T(8,128)S(1)} %copy-done.15), custom_call_target="tpu_custom_call" | custom-call | tf_op jit(solution)/shard_map/pallas_call | solution.py:152
  144.4 0.1 copy.49.r_ref
  144.5 1.0 copy.48
  145.5 0.0 copy-start.20
  145.5 7.9 %shard_map.196 = f32[4,2,8,22,168]{4,3,2,1,0:T(8,128)S(1)} custom-call(s32[8]{0:T(128)S(1)} %dynamic_slice.6.oct_ref, f32[4,2,2,40,312]{4,3,2,1,0:T(8,128)S(1)} %shard_map.195.g_ref, f32[88,160]{1,0:T(8,128)S(1)} %bitcast.29, f32[312,168]{1,0:T(8,128)S(1)} %copy.49.r_ref, f32[8,160,312]{2,1,0:T(8,128)S(1)} %copy-done.1), custom_call_target="tpu_custom_call" | custom-call | tf_op jit(solution)/shard_map/pallas_call | solution.py:152
  153.5 0.0 copy-start.4
  153.5 1.1 copy-done.4
  154.6 0.0 copy-done.20
  154.7 0.1 copy.42
  154.8 1.6 copy.50
  156.4 0.1 copy.51.o_ref
  156.5 23.9 %shard_map.197 = f32[64,22,168]{2,1,0:T(8,128)S(1)} custom-call(s32[32,16]{1,0:T(8,128)S(1)} %fusion.2.e_ref, s32[32,16]{1,0:T(8,128)S(1)} %copy.51.o_ref, s32[32]{0:T(128)S(1)} %fusion.18.at_ref, f32[64,22,168]{2,1,0:T(8,128)S(1)} %bitcast.23, f32[192,22,168]{2,1,0:T(8,128)} %bitcast.32, f32[32,22,168]{2,1,0:T(8,128)S(1)} %bitcast.26), custom_call_target="tpu_custom_call" | custom-call | tf_op jit(solution)/shard_map/pallas_call | solution.py:392
  180.4 1.5 copy.52
  (28 shorter events, 0.1 us)
Async XLA Ops:
  0.0 63.7 %copy-start = (s32[8,16]{1,0:T(8,128)S(1)}, s32[8,16]{1,0:T(8,128)}, u32[]{:S(2)}) copy-start(s32[8,16]{1,0:T(8,128)} %param.38) | copy-start | bytes 1540
  6.0 1.4 copy-start.19
  8.2 21.2 %copy-start.1 = (f32[8,160,312]{2,1,0:T(8,128)S(1)}, f32[8,160,312]{2,1,0:T(8,128)}, u32[]{:S(2)}) copy-start(f32[8,160,312]{2,1,0:T(8,128)} %shift_ref.7) | copy-start | bytes 4792324
  8.2 21.2 %copy-start.13 = (f32[312,168]{0,1:T(8,128)S(1)}, f32[312,168]{0,1:T(8,128)}, u32[]{:S(2)}) copy-start(f32[312,168]{0,1:T(8,128)} %param.22) | copy-start | bytes 628996
  8.2 21.2 %copy-start.17 = (f32[160,88]{1,0:T(8,128)S(1)}, f32[160,88]{1,0:T(8,128)}, u32[]{:S(2)}) copy-start(f32[160,88]{1,0:T(8,128)} %q_ref.2) | copy-start | bytes 168964
  29.4 7.8 %copy-start.24 = (s32[8]{0:T(128)S(1)}, s32[8]{0:T(128)}, u32[]{:S(2)}) copy-start(s32[8]{0:T(128)} %param.28) | copy-start | bytes 100
  38.5 1.1 copy-start.9
  46.3 1.2 copy-start.2
  47.5 15.6 %copy-start.22 = (s32[8,16]{1,0:T(8,128)S(1)}, s32[8,16]{1,0:T(8,128)}, u32[]{:S(2)}) copy-start(s32[8,16]{1,0:T(8,128)} %param.35) | copy-start | bytes 1540
  47.5 16.8 %copy-start.23 = (s32[2,16]{1,0:T(2,128)S(1)}, s32[2,16]{1,0:T(2,128)}, u32[]{:S(2)}) copy-start(s32[2,16]{1,0:T(2,128)} %param.36) | copy-start | bytes 388
  62.1 0.9 copy-start.6
  64.3 7.5 %copy-start.3 = (f32[4,2,1,74,584]{4,3,2,1,0:T(8,128)S(1)}, f32[4,2,1,74,584]{4,3,2,1,0:T(8,128)}, u32[]{:S(2)}) copy-start(f32[4,2,1,74,584]{4,3,2,1,0:T(8,128)} %copy-done.2) | copy-start | bytes 4148740
  64.3 7.5 %copy-start.7 = (f32[4,2,2,40,312]{4,3,2,1,0:T(8,128)S(1)}, f32[4,2,2,40,312]{4,3,2,1,0:T(8,128)}, u32[]{:S(2)}) copy-start(f32[4,2,2,40,312]{4,3,2,1,0:T(8,128)} %copy-done.6) | copy-start | bytes 2396164
  64.3 7.5 %copy-start.18 = (s32[2,16]{1,0:T(2,128)S(1)}, s32[2,16]{1,0:T(2,128)}, u32[]{:S(2)}) copy-start(s32[2,16]{1,0:T(2,128)} %o_top.1) | copy-start | bytes 388
  71.7 60.6 %copy-start.10 = (f32[584,312]{0,1:T(8,128)S(1)}, f32[584,312]{0,1:T(8,128)}, u32[]{:S(2)}) copy-start(f32[584,312]{0,1:T(8,128)} %param.24) | copy-start | bytes 2186500
  130.2 1.2 copy-start.11
  131.4 0.9 copy-start.14
  132.3 1.3 copy-start.16
  133.6 1.2 copy-start.8
  134.8 1.4 copy-start.12
  136.2 1.2 copy-start.15
  145.5 9.1 %copy-start.20 = (s32[32,16]{0,1:T(8,128)S(1)}, s32[32,16]{0,1:T(8,128)}, u32[]{:S(2)}) copy-start(s32[32,16]{0,1:T(8,128)} %param.34) | copy-start | bytes 6148
  153.5 1.2 copy-start.4
  154.6 1.8 copy-start.21
  154.6 1.9 %copy-start.5 = (f32[4,2,8,22,168]{4,3,2,1,0:T(8,128)S(1)}, f32[4,2,8,22,168]{4,3,2,1,0:T(8,128)}, u32[]{:S(2)}) copy-start(f32[4,2,8,22,168]{4,3,2,1,0:T(8,128)} %copy-done.4) | copy-start | bytes 2838532

commit v3 on v2

--- a/solution.py
+++ b/solution.py
@@ -7,7 +7,7 @@
 from jax.experimental.pallas import tpu as pltpu
 from jax.sharding import PartitionSpec as P
 
-VMEM_LIMIT = 48 * 1024 * 1024
+MIB = 1024 * 1024
 VMEM = pltpu.VMEM
 SMEM = pltpu.SMEM
 
@@ -92,7 +92,7 @@
         functools.partial(up_kernel, n, kids),
         grid_spec=spec,
         out_shape=jax.ShapeDtypeStruct((n, 2, parents, s // n, q), jnp.float32),
-        compiler_params=pltpu.CompilerParams(vmem_limit_bytes=VMEM_LIMIT),
+        compiler_params=pltpu.CompilerParams(vmem_limit_bytes=24 * MIB),
     )(octant, x, theta_w, phi_w.T, angles)
 
 
@@ -153,7 +153,7 @@
         functools.partial(down_kernel, n, kids, with_add),
         grid_spec=spec,
         out_shape=jax.ShapeDtypeStruct((n, 2, boxes, t // n, p), jnp.float32),
-        compiler_params=pltpu.CompilerParams(vmem_limit_bytes=VMEM_LIMIT),
+        compiler_params=pltpu.CompilerParams(vmem_limit_bytes=24 * MIB),
     )(*args)
 
 
@@ -237,9 +237,9 @@
 
 
 def middle_kernel(
-    n, runs, e_mid, o_mid, rank, e_top, o_top, top_parts, mid_rows, tab_mid, tab_top,
-    top_here, mid_here, near_mid, near_top, top_rows, in_mid, in_top,
-    send, recv, halo_send, halo_recv,
+    n, runs, e_mid, o_mid, rank, e_top, o_top, octant, mid_parts, tab_mid, tab_top,
+    theta, phi_t, angles, top_here, mid_here, near_mid, near_top, top_rows, in_mid, in_top,
+    mid_rows, top_parts, x_all, mixed, send, recv, halo_send, halo_recv,
 ):
     me = lax.axis_index("samp")
     mids, tops = e_mid.shape[0], e_top.shape[0]
@@ -258,7 +258,27 @@
             copy.start()
         return copies
 
+    mids_up = swap(3, mid_parts, mid_rows, 1)
+    mid_rows[me] = mid_parts[me]
+    rows, rows_top = mid_parts.shape[3], top_parts.shape[3]
+    full = n * rows
+    for i in range(each):
+        for r in range(2):
+            for k in range(n):
+                x_all[r * full + k * rows:r * full + (k + 1) * rows, :] = mid_parts[k, r, i]
+        interp = dot3(x_all[...], phi_t[...])
+        real = dot3(theta[...], interp[:full])
+        imag = dot3(theta[...], interp[full:])
+        sine, cosine = sincos(angles[octant[i]])
+        turned = (real * cosine - imag * sine, real * sine + imag * cosine)
+        for r in range(2):
+            mixed[r] = turned[r] if i == 0 else mixed[r] + turned[r]
+    for r in range(2):
+        for k in range(n):
+            top_parts[k, r, 0] = mixed[r, k * rows_top:(k + 1) * rows_top, :]
     tops_out = swap(0, top_parts, top_rows, 1)
+    for copy in mids_up:
+        copy.wait()
 
     def natural(b, carry):
         place = rank[b]
@@ -318,31 +338,42 @@
     return x.reshape((-1,) + x.shape[lead:])
 
 
-def middle_stage(number, mid_rows, top_parts, rank, trans_mid, trans_top, e_mid, o_mid, e_top, o_top):
+def middle_stage(
+    number, mid_parts, octant, theta_w, phi_w, angles, rank, trans_mid, trans_top,
+    e_mid, o_mid, e_top, o_top,
+):
     n, runs = lax.axis_size("samp"), lax.axis_size("box")
     mids, tops = e_mid.shape[0], e_top.shape[0]
     f32, dma = jnp.float32, pltpu.SemaphoreType.DMA
-    row_mid, row_top = mid_rows.shape[3:], top_parts.shape[3:]
+    s, q = theta_w.shape[0], phi_w.shape[0]
+    row_mid, row_top = mid_parts.shape[3:], (s // n, q)
+    top_shape = (n, 2, 1) + row_top
     spec = pl.BlockSpec(memory_space=VMEM)
     return pl.pallas_call(
         functools.partial(middle_kernel, n, runs),
-        in_specs=[pl.BlockSpec(memory_space=SMEM)] * 5 + [spec] * 4,
+        in_specs=[pl.BlockSpec(memory_space=SMEM)] * 6 + [spec] * 6,
         out_specs=[spec, spec],
         out_shape=[
-            jax.ShapeDtypeStruct(top_parts.shape, f32),
-            jax.ShapeDtypeStruct(mid_rows.shape, f32),
+            jax.ShapeDtypeStruct(top_shape, f32),
+            jax.ShapeDtypeStruct(mid_parts.shape, f32),
         ],
         scratch_shapes=[
             pltpu.VMEM((6 * mids,) + row_mid, f32),
             pltpu.VMEM((6 * tops,) + row_top, f32),
-            pltpu.VMEM(top_parts.shape, f32),
-            pltpu.VMEM(mid_rows.shape, f32),
+            pltpu.VMEM(top_shape, f32),
+            pltpu.VMEM(mid_parts.shape, f32),
             pltpu.VMEM((tops, 2, 1) + row_top, f32),
-            dma((3, n)), dma((3, n)), dma((2, 2)), dma((2, 2)),
+            pltpu.VMEM(mid_parts.shape, f32),
+            pltpu.VMEM(top_shape, f32),
+            pltpu.VMEM((2 * theta_w.shape[1], phi_w.shape[1]), f32),
+            pltpu.VMEM((2, s, q), f32),
+            dma((4, n)), dma((4, n)), dma((2, 2)), dma((2, 2)),
         ],
         compiler_params=pltpu.CompilerParams(
-            collective_id=number, has_side_effects=True, vmem_limit_bytes=VMEM_LIMIT),
-    )(e_mid, o_mid, rank, e_top, o_top, top_parts, mid_rows, flat(trans_mid, 2), flat(trans_top, 2))
+            collective_id=number, has_side_effects=True, vmem_limit_bytes=40 * MIB),
+    )(
+        e_mid, o_mid, rank, e_top, o_top, octant, mid_parts, flat(trans_mid, 2),
+        flat(trans_top, 2), theta_w, phi_w.T, angles)
 
 
 def last_kernel(n, runs, e_ref, o_ref, at_ref, low_in, pat, tab, out_ref, landed, send, recv):
@@ -396,7 +427,7 @@
         out_shape=jax.ShapeDtypeStruct((2 * boxes,) + row, jnp.float32),
         scratch_shapes=[pltpu.VMEM((2 * boxes,) + row, jnp.float32), dma((n,)), dma((n,))],
         compiler_params=pltpu.CompilerParams(
-            collective_id=number, has_side_effects=True, vmem_limit_bytes=VMEM_LIMIT),
+            collective_id=number, has_side_effects=True, vmem_limit_bytes=32 * MIB),
     )(e_low, o_low, place, flat(low_in, 3), flat(near, 3), flat(table, 2)).reshape((2, boxes) + row)
 
 
@@ -483,7 +514,7 @@
             dma((max(len(halos), 1), 2)),
         ],
         compiler_params=pltpu.CompilerParams(
-            collective_id=number, has_side_effects=True, vmem_limit_bytes=VMEM_LIMIT),
+            collective_id=number, has_side_effects=True, vmem_limit_bytes=8 * MIB),
     )(*arrays)
 
 
@@ -522,10 +553,8 @@
     grouped = jnp.moveaxis(grouped.reshape(2, n, low_each, rows_low, p_low), 1, 0)
     low_parts, near_low = exchange(0, [(grouped, 1)], [radiation])
     mid_parts = go_up(low_parts, theta_mid, phi_mid, shift_mid, oct_low, mid_each)
-    mid_rows, = exchange(1, [(mid_parts, 1)], [])
-    top_parts = go_up(mid_parts, theta_top, phi_top, shift_top, oct_mid, 1)
     top_here, mid_here = middle_stage(
-        2, mid_rows, top_parts, rank_mid, trans_mid, trans_top,
+        2, mid_parts, oct_mid, theta_top, phi_top, shift_top, rank_mid, trans_mid, trans_top,
         entries(far_mid, mids)[order_mid], offset_mid[order_mid],
         entries(far_top, tops), offset_top)
     mid_in = go_down(top_here, theta_top, phi_top, shift_top, oct_mid, mid_here)

time: 183 us -> 183 us (level)
  Pallas kernels: 147 us -> 135 us
  local copies, waits for them, and re-layouts: 30.2 us -> 41.8 us
    pallas_call x2 -> x1, Pallas kernels: 35.8 us -> 21.1 us  [exchange(): pl.pallas_call(functools.partial(exchange_kernel, n, runs, len(swaps), le...]
    pallas_call x1, Pallas kernels: 58.5 us -> 71.6 us  [middle_stage(): pl.pallas_call(functools.partial(middle_kernel, n, runs), in_specs=[pl.Bl...]
    unnamed x59 -> x67, local copies, waits for them, and re-layouts: 24.2 us -> 35.8 us
    pallas_call x2 -> x1, Pallas kernels: 14.2 us -> 7.65 us  [go_up(): pl.pallas_call(functools.partial(up_kernel, n, kids), grid_spec=spec, out...]
    pallas_call x1, Pallas kernels: 23.9 us -> 20.9 us  [last_stage(): pl.pallas_call(functools.partial(last_kernel, n, runs), in_specs=[pl.Bloc...]
where the time goes in v3:
time: 183 us; the launch traced here: 181 us
  Pallas kernels  135 us (74%)
  local copies, waits for them, and re-layouts  41.8 us (23%)
  other arithmetic  4.15 us (2%)
    pallas_call x1, Pallas kernels, middle_stage(): pl.pallas_call(functools.partial(middle_kernel, n, runs), in_specs=[pl.Bl...  71.6 us
    unnamed x67, local copies, waits for them, and re-layouts  35.8 us
    pallas_call x1, Pallas kernels, exchange(): pl.pallas_call(functools.partial(exchange_kernel, n, runs, len(swaps), le...  21.1 us
    pallas_call x1, Pallas kernels, last_stage(): pl.pallas_call(functools.partial(last_kernel, n, runs), in_specs=[pl.Bloc...  20.9 us
    pallas_call x2, Pallas kernels, go_down(): pl.pallas_call(functools.partial(down_kernel, n, kids, with_add), grid_sp...  13.8 us
    pallas_call x1, Pallas kernels, go_up(): pl.pallas_call(functools.partial(up_kernel, n, kids), grid_spec=spec, out...  7.65 us

profile of v3, /device:TPU:8, one launch (start us, length us, event | category | flops | bytes accessed | tf_op | source)
XLA Modules:
  0.0 181.4 jit_solution(13034378244735721472)
XLA Ops:
  0.0 0.0 copy-start
  0.0 0.7 broadcast_subtract_fusion
  0.7 0.9 convert_reduce_fusion.1.rank
  1.6 0.1 select_reduce_fusion.4
  1.7 0.2 convert_reduce_fusion
  1.9 0.1 select_reduce_fusion.1
  2.0 0.8 select_reduce_fusion
  2.8 0.1 dynamic_slice.6.oct_ref
  2.9 3.1 %gather_fusion.2 = f32[32,2,22,168]{3,0,2,1:T(8,128)S(1)} fusion(f32[2,32,22,168]{3,1,2,0:T(8,128)} %param.20, s32[1024]{0:T(1024)S(1)} %pad_clamp_fusion), kind=kCustom, calls=%fused_computation.2 | custom fusion | bytes 1892480 | tf_op jit(solution)/shard_map/jit(_take)/gather | solution.py:552
  6.0 0.0 copy-start.21
  6.0 0.1 reduce_sum.77
  6.1 0.9 fusion.refs_0_
  7.1 0.3 copy-done.21
  7.4 0.8 copy.44.refs_1_
  8.2 0.0 copy-start.3
  8.2 0.0 copy-start.13
  8.2 0.0 copy-start.18
  8.2 21.1 %shard_map.190 = (f32[4,2,8,22,168]{4,3,2,1,0:T(8,128)S(1)}, f32[3,2,32,22,168]{4,3,2,1,0:T(8,128)S(1)}) custom-call(f32[4,2,8,22,168]{4,3,2,1,0:T(8,128)S(1)} %fusion.refs_0_, f32[2,32,22,168]{3,2,1,0:T(8,128)S(1)} %copy.44.refs_1_), custom_call_target="tpu_custom_call" | custom-call | tf_op jit(solution)/shard_map/pallas_call | solution.py:503
  29.4 2.2 %copy-done.4 = f32[3,2,32,22,168]{4,3,2,1,0:T(8,128)} copy-done((f32[3,2,32,22,168]{4,3,2,1,0:T(8,128)}, f32[3,2,32,22,168]{4,3,2,1,0:T(8,128)S(1)}, u32[]{:S(2)}) %copy-start.4) | copy-done | bytes 2838552
  31.6 0.0 copy-done.3
  31.6 0.0 copy-done.18
  31.6 0.0 copy-start.24
  31.7 0.0 copy-start.25
  31.7 7.6 %shard_map.191.mid_parts = f32[4,2,2,40,312]{4,3,2,1,0:T(8,128)S(1)} custom-call(s32[8]{0:T(128)S(1)} %dynamic_slice.6.oct_ref, f32[4,2,8,22,168]{4,3,2,1,0:T(8,128)S(1)} %get-tuple-element.9.x_ref, f32[160,88]{1,0:T(8,128)S(1)} %copy-done.18, f32[168,312]{1,0:T(8,128)S(1)} %bitcast.29, f32[8,160,312]{2,1,0:T(8,128)S(1)} %copy-done.3), custom_call_target="tpu_custom_call" | custom-call | tf_op jit(solution)/shard_map/pallas_call | solution.py:91
  39.3 0.1 select_reduce_fusion.3
  39.4 0.2 select_reduce_fusion.2
  39.6 0.1 dynamic_slice.7.octant.oct_ref
  39.7 0.0 copy-done.24
  39.7 0.6 gather_fusion
  40.3 0.0 copy-done
  40.3 0.6 gather_fusion.1
  40.9 0.0 copy-start.20
  40.9 7.3 %copy.45 = f32[2,16,74,584]{3,2,1,0:T(8,128)} copy(f32[2,16,74,584]{3,1,2,0:T(8,128)} %param.33) | data formatting | bytes 11063296 | tf_op args[13]
  48.2 1.1 copy.46.theta
  49.3 0.0 copy-done.20
  49.3 0.0 copy-start.1
  49.3 2.7 %copy-done.1 = f32[8,296,584]{2,1,0:T(8,128)S(1)} copy-done((f32[8,296,584]{2,1,0:T(8,128)S(1)}, f32[8,296,584]{2,1,0:T(8,128)}, u32[]{:S(2)}) %copy-start.1) | copy-done | bytes 5531672
  52.0 1.1 copy-done.8
  53.2 1.5 copy-done.9
  54.7 71.6 %shard_map.192 = (f32[4,2,1,74,584]{4,3,2,1,0:T(8,128)S(1)}, f32[4,2,2,40,312]{4,3,2,1,0:T(8,128)S(1)}) custom-call(s32[8,16]{1,0:T(8,128)S(1)} %gather_fusion, s32[8,16]{1,0:T(8,128)S(1)} %gather_fusion.1, s32[8]{0:T(128)S(1)} %convert_reduce_fusion.1.rank, s32[2,16]{1,0:T(2,128)S(1)} %fusion.17.e_top, s32[2,16]{1,0:T(2,128)S(1)} %copy-done.20, ...), custom_call_target="tpu_custom_call" | custom-call | tf_op jit(solution)/shard_map/pallas_call | solution.py:352
  126.3 1.2 copy-done.10
  127.5 0.9 copy-done.14
  128.4 1.5 copy.47.r_ref
  129.9 0.0 copy-start.2
  129.9 2.7 %copy-done.2 = f32[8,296,584]{2,1,0:T(8,128)S(1)} copy-done((f32[8,296,584]{2,1,0:T(8,128)S(1)}, f32[8,296,584]{2,1,0:T(8,128)}, u32[]{:S(2)}) %copy-start.2) | copy-done | bytes 5531672
  132.7 1.4 copy-done.11
  134.1 1.2 copy-done.15
  135.3 5.9 %shard_map.193.g_ref = f32[4,2,2,40,312]{4,3,2,1,0:T(8,128)S(1)} custom-call(s32[2]{0:T(128)S(1)} %dynamic_slice.7.octant.oct_ref, f32[4,2,1,74,584]{4,3,2,1,0:T(8,128)S(1)} %copy-done.11, f32[160,296]{1,0:T(8,128)S(1)} %bitcast.30, f32[584,312]{1,0:T(8,128)S(1)} %copy.47.r_ref, f32[8,296,584]{2,1,0:T(8,128)S(1)} %copy-done.2, ...), custom_call_target="tpu_custom_call" | custom-call | tf_op jit(solution)/shard_map/pallas_call | solution.py:152
  141.2 0.0 copy-start.6
  141.2 0.9 copy-done.6
  142.1 0.9 copy.49.r_ref
  143.0 0.7 copy.48
  143.8 1.2 copy-done.7
  145.0 1.0 copy-done.12
  145.9 0.9 copy-done.17
  146.8 7.9 %shard_map.194 = f32[4,2,8,22,168]{4,3,2,1,0:T(8,128)S(1)} custom-call(s32[8]{0:T(128)S(1)} %dynamic_slice.6.oct_ref, f32[4,2,2,40,312]{4,3,2,1,0:T(8,128)S(1)} %copy-done.7, f32[88,160]{1,0:T(8,128)S(1)} %bitcast.31, f32[312,168]{1,0:T(8,128)S(1)} %copy-done.12, f32[8,160,312]{2,1,0:T(8,128)S(1)} %copy-done.3), custom_call_target="tpu_custom_call" | custom-call | tf_op jit(solution)/shard_map/pallas_call | solution.py:152
  154.8 0.0 copy-start.23
  154.8 0.1 copy.42
  154.9 1.5 copy.50
  156.5 0.0 copy-done.23
  156.5 0.1 copy.51.o_ref
  156.6 2.3 %copy-done.5 = f32[3,2,32,22,168]{4,3,2,1,0:T(8,128)S(1)} copy-done((f32[3,2,32,22,168]{4,3,2,1,0:T(8,128)S(1)}, f32[3,2,32,22,168]{4,3,2,1,0:T(8,128)}, u32[]{:S(2)}) %copy-start.5) | copy-done | bytes 2838552
  158.9 20.9 %shard_map.195 = f32[64,22,168]{2,1,0:T(8,128)S(1)} custom-call(s32[32,16]{1,0:T(8,128)S(1)} %fusion.2.e_ref, s32[32,16]{1,0:T(8,128)S(1)} %copy.51.o_ref, s32[32]{0:T(128)S(1)} %fusion.18.at_ref, f32[64,22,168]{2,1,0:T(8,128)S(1)} %bitcast.23, f32[192,22,168]{2,1,0:T(8,128)S(1)} %bitcast.25, f32[32,22,168]{2,1,0:T(8,128)S(1)} %bitcast.27), custom_call_target="tpu_custom_call" | custom-call | tf_op jit(solution)/shard_map/pallas_call | solution.py:423
  179.8 1.5 copy.52
  (34 shorter events, 0.1 us)
Async XLA Ops:
  0.0 40.3 %copy-start = (s32[8,16]{1,0:T(8,128)S(1)}, s32[8,16]{1,0:T(8,128)}, u32[]{:S(2)}) copy-start(s32[8,16]{1,0:T(8,128)} %param.38) | copy-start | bytes 1540
  1.9 1.0 copy-start.27
  6.0 1.4 copy-start.21
  8.2 23.4 %copy-start.3 = (f32[8,160,312]{2,1,0:T(8,128)S(1)}, f32[8,160,312]{2,1,0:T(8,128)}, u32[]{:S(2)}) copy-start(f32[8,160,312]{2,1,0:T(8,128)} %shift_ref.5) | copy-start | bytes 4792324
  8.2 23.4 %copy-start.13 = (f32[312,168]{0,1:T(8,128)S(1)}, f32[312,168]{0,1:T(8,128)}, u32[]{:S(2)}) copy-start(f32[312,168]{0,1:T(8,128)} %param.22) | copy-start | bytes 628996
  8.2 23.4 %copy-start.18 = (f32[160,88]{1,0:T(8,128)S(1)}, f32[160,88]{1,0:T(8,128)}, u32[]{:S(2)}) copy-start(f32[160,88]{1,0:T(8,128)} %q_ref.1) | copy-start | bytes 168964
  29.4 2.2 %copy-start.4 = (f32[3,2,32,22,168]{4,3,2,1,0:T(8,128)}, f32[3,2,32,22,168]{4,3,2,1,0:T(8,128)S(1)}, u32[]{:S(2)}) copy-start(f32[3,2,32,22,168]{4,3,2,1,0:T(8,128)S(1)} %get-tuple-element.12) | copy-start | bytes 8515588
  31.6 7.8 %copy-start.26 = (s32[8]{0:T(128)S(1)}, s32[8]{0:T(128)}, u32[]{:S(2)}) copy-start(s32[8]{0:T(128)} %param.28) | copy-start | bytes 100
  31.6 8.1 %copy-start.24 = (s32[8,16]{1,0:T(8,128)S(1)}, s32[8,16]{1,0:T(8,128)}, u32[]{:S(2)}) copy-start(s32[8,16]{1,0:T(8,128)} %param.35) | copy-start | bytes 1540
  31.7 9.2 %copy-start.25 = (s32[2,16]{1,0:T(2,128)S(1)}, s32[2,16]{1,0:T(2,128)}, u32[]{:S(2)}) copy-start(s32[2,16]{1,0:T(2,128)} %param.36) | copy-start | bytes 388
  40.9 8.4 %copy-start.20 = (s32[2,16]{1,0:T(2,128)S(1)}, s32[2,16]{1,0:T(2,128)}, u32[]{:S(2)}) copy-start(s32[2,16]{1,0:T(2,128)} %o_top.1) | copy-start | bytes 388
  49.3 2.7 %copy-start.1 = (f32[8,296,584]{2,1,0:T(8,128)S(1)}, f32[8,296,584]{2,1,0:T(8,128)}, u32[]{:S(2)}) copy-start(f32[8,296,584]{2,1,0:T(8,128)} %shift_ref.4) | copy-start | bytes 16594948
  52.0 1.1 copy-start.8
  53.2 1.5 copy-start.9
  126.3 1.2 copy-start.10
  127.5 0.9 copy-start.14
  128.4 1.5 copy-start.16
  129.9 2.7 %copy-start.2 = (f32[8,296,584]{2,1,0:T(8,128)S(1)}, f32[8,296,584]{2,1,0:T(8,128)}, u32[]{:S(2)}) copy-start(f32[8,296,584]{2,1,0:T(8,128)} %shift_ref.4) | copy-start | bytes 16594948
  132.7 1.4 copy-start.11
  134.1 1.2 copy-start.15
  135.3 7.7 %copy-start.19 = (f32[160,88]{1,0:T(8,128)S(1)}, f32[160,88]{1,0:T(8,128)}, u32[]{:S(2)}) copy-start(f32[160,88]{1,0:T(8,128)} %q_ref.1) | copy-start | bytes 168964
  141.2 0.9 copy-start.6
  143.8 1.2 copy-start.7
  145.0 1.0 copy-start.12
  145.9 0.9 copy-start.17
  146.8 8.0 %copy-start.28 = (s32[32]{0:T(128)S(1)}, s32[32]{0:T(128)}, u32[]{:S(2)}) copy-start(s32[32]{0:T(128)} %copy-done.27) | copy-start | bytes 388
  146.8 8.0 %copy-start.22 = (s32[32,16]{0,1:T(8,128)S(1)}, s32[32,16]{0,1:T(8,128)}, u32[]{:S(2)}) copy-start(s32[32,16]{0,1:T(8,128)} %param.34) | copy-start | bytes 6148
  154.8 1.7 copy-start.23
  156.6 2.3 %copy-start.5 = (f32[3,2,32,22,168]{4,3,2,1,0:T(8,128)S(1)}, f32[3,2,32,22,168]{4,3,2,1,0:T(8,128)}, u32[]{:S(2)}) copy-start(f32[3,2,32,22,168]{4,3,2,1,0:T(8,128)} %copy-done.4) | copy-start | bytes 8515588

commit v4 on v3

--- a/solution.py
+++ b/solution.py
@@ -7,7 +7,7 @@
 from jax.experimental.pallas import tpu as pltpu
 from jax.sharding import PartitionSpec as P
 
-MIB = 1024 * 1024
+GRANT = 60 * 1024 * 1024
 VMEM = pltpu.VMEM
 SMEM = pltpu.SMEM
 
@@ -92,7 +92,7 @@
         functools.partial(up_kernel, n, kids),
         grid_spec=spec,
         out_shape=jax.ShapeDtypeStruct((n, 2, parents, s // n, q), jnp.float32),
-        compiler_params=pltpu.CompilerParams(vmem_limit_bytes=24 * MIB),
+        compiler_params=pltpu.CompilerParams(vmem_limit_bytes=GRANT),
     )(octant, x, theta_w, phi_w.T, angles)
 
 
@@ -153,7 +153,7 @@
         functools.partial(down_kernel, n, kids, with_add),
         grid_spec=spec,
         out_shape=jax.ShapeDtypeStruct((n, 2, boxes, t // n, p), jnp.float32),
-        compiler_params=pltpu.CompilerParams(vmem_limit_bytes=24 * MIB),
+        compiler_params=pltpu.CompilerParams(vmem_limit_bytes=GRANT),
     )(*args)
 
 
@@ -370,7 +370,7 @@
             dma((4, n)), dma((4, n)), dma((2, 2)), dma((2, 2)),
         ],
         compiler_params=pltpu.CompilerParams(
-            collective_id=number, has_side_effects=True, vmem_limit_bytes=40 * MIB),
+            collective_id=number, has_side_effects=True, vmem_limit_bytes=GRANT),
     )(
         e_mid, o_mid, rank, e_top, o_top, octant, mid_parts, flat(trans_mid, 2),
         flat(trans_top, 2), theta_w, phi_w.T, angles)
@@ -427,7 +427,7 @@
         out_shape=jax.ShapeDtypeStruct((2 * boxes,) + row, jnp.float32),
         scratch_shapes=[pltpu.VMEM((2 * boxes,) + row, jnp.float32), dma((n,)), dma((n,))],
         compiler_params=pltpu.CompilerParams(
-            collective_id=number, has_side_effects=True, vmem_limit_bytes=32 * MIB),
+            collective_id=number, has_side_effects=True, vmem_limit_bytes=GRANT),
     )(e_low, o_low, place, flat(low_in, 3), flat(near, 3), flat(table, 2)).reshape((2, boxes) + row)
 
 
@@ -514,7 +514,7 @@
             dma((max(len(halos), 1), 2)),
         ],
         compiler_params=pltpu.CompilerParams(
-            collective_id=number, has_side_effects=True, vmem_limit_bytes=8 * MIB),
+            collective_id=number, has_side_effects=True, vmem_limit_bytes=GRANT),
     )(*arrays)
 
 

time: 183 us -> 226 us (1.23)
  Pallas kernels: 135 us -> 193 us
  local copies, waits for them, and re-layouts: 41.8 us -> 24.7 us
  other arithmetic: 4.15 us -> 7.01 us
    pallas_call x1, Pallas kernels: 21.1 us -> 63.2 us  [exchange(): pl.pallas_call(functools.partial(exchange_kernel, n, runs, len(swaps), le...]
    unnamed x67 -> x35, local copies, waits for them, and re-layouts: 35.8 us -> 15.1 us
    pallas_call x2, Pallas kernels: 13.8 us -> 19.5 us  [go_down(): pl.pallas_call(functools.partial(down_kernel, n, kids, with_add), grid_sp...]
    pallas_call x1, Pallas kernels: 71.6 us -> 75.3 us  [middle_stage(): pl.pallas_call(functools.partial(middle_kernel, n, runs), in_specs=[pl.Bl...]
    pallas_call x1, Pallas kernels: 20.9 us -> 24.4 us  [last_stage(): pl.pallas_call(functools.partial(last_kernel, n, runs), in_specs=[pl.Bloc...]
    pallas_call x1, Pallas kernels: 7.65 us -> 10.6 us  [go_up(): pl.pallas_call(functools.partial(up_kernel, n, kids), grid_spec=spec, out...]
where the time goes in v4:
time: 226 us; the launch traced here: 225 us
  Pallas kernels  193 us (85%)
  local copies, waits for them, and re-layouts  24.7 us (11%)
  other arithmetic  7.01 us (3%)
    pallas_call x1, Pallas kernels, middle_stage(): pl.pallas_call(functools.partial(middle_kernel, n, runs), in_specs=[pl.Bl...  75.3 us
    pallas_call x1, Pallas kernels, exchange(): pl.pallas_call(functools.partial(exchange_kernel, n, runs, len(swaps), le...  63.2 us
    pallas_call x1, Pallas kernels, last_stage(): pl.pallas_call(functools.partial(last_kernel, n, runs), in_specs=[pl.Bloc...  24.4 us
    pallas_call x2, Pallas kernels, go_down(): pl.pallas_call(functools.partial(down_kernel, n, kids, with_add), grid_sp...  19.5 us
    unnamed x35, local copies, waits for them, and re-layouts  15.1 us
    pallas_call x1, Pallas kernels, go_up(): pl.pallas_call(functools.partial(up_kernel, n, kids), grid_spec=spec, out...  10.6 us

profile of v4, /device:TPU:8, one launch (start us, length us, event | category | flops | bytes accessed | tf_op | source)
XLA Modules:
  0.0 224.8 jit_solution(12878768326343973764)
XLA Ops:
  0.0 0.0 copy-start
  0.0 0.7 broadcast_subtract_fusion
  0.7 0.9 convert_reduce_fusion.1.rank
  1.6 0.0 copy-start.11
  1.6 0.1 select_reduce_fusion.4
  1.7 0.2 convert_reduce_fusion
  1.9 0.1 select_reduce_fusion.1
  2.0 0.8 select_reduce_fusion
  2.8 0.6 dynamic_slice.6.oct_ref
  3.5 3.1 %gather_fusion.2 = f32[32,2,22,168]{3,0,2,1:T(8,128)S(1)} fusion(f32[2,32,22,168]{3,1,2,0:T(8,128)} %param.20, s32[1024]{0:T(1024)S(1)} %pad_clamp_fusion), kind=kCustom, calls=%fused_computation.2 | custom fusion | bytes 1892480 | tf_op jit(solution)/shard_map/jit(_take)/gather | solution.py:552
  6.6 0.0 copy-start.1
  6.6 0.1 reduce_sum.77
  6.7 2.1 fusion.refs_0_
  8.8 0.0 copy-done.1
  8.8 2.0 copy.44.refs_1_
  10.8 63.2 %shard_map.190 = (f32[4,2,8,22,168]{4,3,2,1,0:T(8,128)}, f32[3,2,32,22,168]{4,3,2,1,0:T(8,128)}) custom-call(f32[4,2,8,22,168]{4,3,2,1,0:T(8,128)} %fusion.refs_0_, f32[2,32,22,168]{3,2,1,0:T(8,128)} %copy.44.refs_1_), custom_call_target="tpu_custom_call" | custom-call | tf_op jit(solution)/shard_map/pallas_call | solution.py:503
  74.0 0.0 copy-start.12
  74.0 0.0 copy-start.9
  74.0 0.0 copy-start.10
  74.0 10.6 %shard_map.191.mid_parts = f32[4,2,2,40,312]{4,3,2,1,0:T(8,128)} custom-call(s32[8]{0:T(128)} %dynamic_slice.6.oct_ref, f32[4,2,8,22,168]{4,3,2,1,0:T(8,128)} %get-tuple-element.9.x_ref, f32[160,88]{1,0:T(8,128)} %q_ref.1, f32[168,312]{1,0:T(8,128)} %bitcast.31, f32[8,160,312]{2,1,0:T(8,128)} %shift_ref.5), custom_call_target="tpu_custom_call" | custom-call | tf_op jit(solution)/shard_map/pallas_call | solution.py:91
  84.6 0.0 copy-done.11
  84.6 0.1 select_reduce_fusion.3
  84.7 0.0 copy-done.12
  84.7 0.2 select_reduce_fusion.2
  84.9 0.6 dynamic_slice.7.octant.oct_ref
  85.5 0.0 copy-done.9
  85.6 1.1 gather_fusion
  86.7 0.0 copy-done
  86.7 1.1 gather_fusion.1
  87.9 0.0 copy-done.10
  87.9 0.5 fusion.17.e_top
  88.4 0.0 copy-start.4
  88.4 7.3 %copy.45 = f32[2,16,74,584]{3,2,1,0:T(8,128)} copy(f32[2,16,74,584]{3,1,2,0:T(8,128)} %param.33) | data formatting | bytes 11063296 | tf_op args[13]
  95.7 0.0 copy-done.4
  95.7 0.8 copy.46.theta
  96.6 0.0 copy-start.2
  96.6 75.3 %shard_map.192 = (f32[4,2,1,74,584]{4,3,2,1,0:T(8,128)}, f32[4,2,2,40,312]{4,3,2,1,0:T(8,128)}) custom-call(s32[8,16]{1,0:T(8,128)} %gather_fusion, s32[8,16]{1,0:T(8,128)} %gather_fusion.1, s32[8]{0:T(128)} %copy-done.11, s32[2,16]{1,0:T(2,128)} %fusion.17.e_top, s32[2,16]{1,0:T(2,128)} %o_top.1, s32[2]{0:T(128)} %dynamic_slice.7.octant.oct_ref, ...), custom_call_target="tpu_custom_call" | custom-call | tf_op jit(solution)/shard_map/pallas_call | solution.py:352
  171.9 0.0 copy-done.2
  171.9 1.2 copy.47.r_ref
  173.1 0.0 copy-start.3
  173.2 0.0 copy-start.6
  173.2 8.9 %shard_map.193.g_ref = f32[4,2,2,40,312]{4,3,2,1,0:T(8,128)} custom-call(s32[2]{0:T(128)} %dynamic_slice.7.octant.oct_ref, f32[4,2,1,74,584]{4,3,2,1,0:T(8,128)} %get-tuple-element.10.g_ref, f32[160,296]{1,0:T(8,128)} %bitcast.32, f32[584,312]{1,0:T(8,128)} %copy.47.r_ref, f32[8,296,584]{2,1,0:T(8,128)} %shift_ref.4, ...), custom_call_target="tpu_custom_call" | custom-call | tf_op jit(solution)/shard_map/pallas_call | solution.py:152
  182.1 0.0 copy-done.3
  182.1 0.9 copy.49.r_ref
  183.0 0.0 copy-done.6
  183.0 0.7 copy.48
  183.7 0.0 copy-start.7
  183.7 0.0 copy-start.5
  183.7 10.5 %shard_map.194 = f32[4,2,8,22,168]{4,3,2,1,0:T(8,128)} custom-call(s32[8]{0:T(128)} %dynamic_slice.6.oct_ref, f32[4,2,2,40,312]{4,3,2,1,0:T(8,128)} %shard_map.193.g_ref, f32[88,160]{1,0:T(8,128)} %bitcast.33, f32[312,168]{1,0:T(8,128)} %copy.49.r_ref, f32[8,160,312]{2,1,0:T(8,128)} %shift_ref.5), custom_call_target="tpu_custom_call" | custom-call | tf_op jit(solution)/shard_map/pallas_call | solution.py:152
  194.2 0.0 copy-start.8
  194.2 0.6 fusion.18.at_ref
  194.8 0.0 copy-done.7
  194.8 0.1 copy.42
  194.9 0.6 fusion.2.e_ref
  195.5 0.0 copy-done.5
  195.5 1.3 copy.50
  196.8 0.0 copy-done.8
  196.8 0.7 copy.51.o_ref
  197.5 24.4 %shard_map.195 = f32[64,22,168]{2,1,0:T(8,128)} custom-call(s32[32,16]{1,0:T(8,128)} %fusion.2.e_ref, s32[32,16]{1,0:T(8,128)} %copy.51.o_ref, s32[32]{0:T(128)} %fusion.18.at_ref, f32[64,22,168]{2,1,0:T(8,128)} %bitcast.25, f32[192,22,168]{2,1,0:T(8,128)} %bitcast.27, f32[32,22,168]{2,1,0:T(8,128)} %bitcast.29), custom_call_target="tpu_custom_call" | custom-call | tf_op jit(solution)/shard_map/pallas_call | solution.py:423
  221.9 2.9 %copy.52 = f32[2,32,22,168]{3,1,2,0:T(8,128)} copy(f32[2,32,22,168]{3,2,1,0:T(8,128)} %bitcast.26) | data formatting | bytes 1892352 | tf_op jit(solution)/shard_map/reshape | solution.py:431
  (6 shorter events, 0.0 us)
Async XLA Ops:
  0.0 86.7 %copy-start = (s32[8,16]{1,0:T(8,128)S(1)}, s32[8,16]{1,0:T(8,128)}, u32[]{:S(2)}) copy-start(s32[8,16]{1,0:T(8,128)} %param.38) | copy-start | bytes 1540
  1.6 83.0 %copy-start.11 = (s32[8]{0:T(128)}, s32[8]{0:T(128)S(1)}, u32[]{:S(2)}) copy-start(s32[8]{0:T(128)S(1)} %convert_reduce_fusion.1.rank) | copy-start | bytes 100
  6.6 2.2 copy-start.1
  74.0 10.7 %copy-start.12 = (s32[8]{0:T(128)S(1)}, s32[8]{0:T(128)}, u32[]{:S(2)}) copy-start(s32[8]{0:T(128)} %param.28) | copy-start | bytes 100
  74.0 11.5 %copy-start.9 = (s32[8,16]{1,0:T(8,128)S(1)}, s32[8,16]{1,0:T(8,128)}, u32[]{:S(2)}) copy-start(s32[8,16]{1,0:T(8,128)} %param.35) | copy-start | bytes 1540
  74.0 13.8 %copy-start.10 = (s32[2,16]{1,0:T(2,128)S(1)}, s32[2,16]{1,0:T(2,128)}, u32[]{:S(2)}) copy-start(s32[2,16]{1,0:T(2,128)} %param.36) | copy-start | bytes 388
  88.4 7.3 %copy-start.4 = (f32[296,160]{0,1:T(8,128)S(1)}, f32[296,160]{0,1:T(8,128)}, u32[]{:S(2)}) copy-start(f32[296,160]{0,1:T(8,128)} %param.23) | copy-start | bytes 568324
  96.6 75.3 %copy-start.2 = (f32[584,312]{0,1:T(8,128)S(1)}, f32[584,312]{0,1:T(8,128)}, u32[]{:S(2)}) copy-start(f32[584,312]{0,1:T(8,128)} %param.24) | copy-start | bytes 2186500
  173.1 9.0 %copy-start.3 = (f32[312,168]{0,1:T(8,128)S(1)}, f32[312,168]{0,1:T(8,128)}, u32[]{:S(2)}) copy-start(f32[312,168]{0,1:T(8,128)} %param.22) | copy-start | bytes 628996
  173.2 9.8 %copy-start.6 = (f32[160,88]{1,0:T(8,128)S(1)}, f32[160,88]{1,0:T(8,128)}, u32[]{:S(2)}) copy-start(f32[160,88]{1,0:T(8,128)} %q_ref.1) | copy-start | bytes 168964
  183.7 11.1 %copy-start.7 = (s32[32,16]{0,1:T(8,128)S(1)}, s32[32,16]{0,1:T(8,128)}, u32[]{:S(2)}) copy-start(s32[32,16]{0,1:T(8,128)} %param.34) | copy-start | bytes 6148
  183.7 11.8 %copy-start.5 = (f32[2,16,22,168]{3,1,2,0:T(8,128)S(1)}, f32[2,16,22,168]{3,1,2,0:T(8,128)}, u32[]{:S(2)}) copy-start(f32[2,16,22,168]{3,1,2,0:T(8,128)} %param.31) | copy-start | bytes 1419268
  194.2 2.6 %copy-start.8 = (s32[32,16]{0,1:T(8,128)S(1)}, s32[32,16]{0,1:T(8,128)}, u32[]{:S(2)}) copy-start(s32[32,16]{0,1:T(8,128)} %param.37) | copy-start | bytes 6148
